TPU v7x, 32 devices: a whole 2x2x4 slice. The times are simulated.
32 devices in a mesh: seq: 8 (over z, y), head: 4 (over x, core).
Axes of the slice: x: 2, y: 2, z: 4, core: 2. Of those that a mesh axis runs over, the one named last changes fastest.
Arguments:
- queries: bfloat16 [4096, 4096], P('seq', 'head'), may hold values from -6 to 6
- key_vectors: bfloat16 [4096, 4096], P('seq', 'head'), may hold values from -6 to 6
- value_vectors: bfloat16 [4096, 4096], P('seq', 'head'), may hold values from -6 to 6
- log_decay: float32 [4096, 32], P('seq', 'head'), may hold values from -0.78 to 0
- head_scale: float32 [32], P('head'), may hold values from 0.2 to 1.6
- send_rows: int32 [8, 2, 128], P('seq'), may hold values from 0 to 511, as said below
- take_rows: int32 [4096], P('seq'), may hold values from 0 to 767, as said below
- doc_lengths: int32 [8], replicated, may hold values from 1 to 1024, as said below
- cotangent: bfloat16 [4096, 4096], P('seq', 'head'), may hold values from -6 to 6
Outputs:
- normed: bfloat16 [4096, 4096], P('seq', 'head')
- grad_queries: bfloat16 [4096, 4096], P('seq', 'head')
- grad_keys: bfloat16 [4096, 4096], P('seq', 'head')
- grad_values: bfloat16 [4096, 4096], P('seq', 'head')
Inputs may be any that keep to these rules, and one draw needn't show every extreme that they name: For shard d, send_rows[d, 0] lists local rows handed to shard d - 1 and send_rows[d, 1] rows handed to shard d + 1; a slot is live only if shard d - 1 (resp. d + 1) takes it; live rows of one shard are distinct over both lists and never a row that take_rows of shard d names among its own; the first shard hands nothing left and the last nothing right. take_rows at a position of shard d indexes [128 rows from shard d - 1, the 512 own rows, 128 rows from shard d + 1]; the values of one shard are distinct and take exactly as many rows from a neighbour as that neighbour hands over; the numbers handed between two neighbours are equal both ways and in every draw some pair hands 128. `doc_lengths`: document lengths sum to 4096; some document other than the first starts at a multiple of 512.
All inputs are finite; a program needn't handle non-finite values.
Results may differ from a plain program's by a relative error of at most 0.0061.
Values may be sent and summed in bfloat16 or wider, within the bound.
No kernel may reach another device: no remote copies, remote signals or barrier semaphores. Data moves between devices by JAX's collectives and lax.ppermute only.
A program may use at most 64 MiB of HBM per device.

v0:
```python
import functools
import math

import jax
import jax.numpy as jnp
from jax import lax
from jax.experimental import pallas as pl
from jax.experimental.pallas import tpu as pltpu
from jax.sharding import PartitionSpec as P

EPSILON = 1e-05
LOG2E = math.log2(math.e)
MASKED = -1e30
VMEM_BYTES = 40 * 1024 * 1024
BF = jnp.bfloat16
F32 = jnp.float32
NT = (((1,), (1,)), ((), ()))
TN = (((0,), (0,)), ((), ()))


def dot(a, b):
    return jnp.dot(a, b, preferred_element_type=F32)


def dot_nt(a, b):
    return lax.dot_general(a, b, NT, preferred_element_type=F32)


def dot_tn(a, b):
    return lax.dot_general(a, b, TN, preferred_element_type=F32)


def along_rows(row, lanes=128):
    return jnp.broadcast_to(row, (lanes, row.shape[1])).T


def iota(shape, dim):
    return lax.broadcasted_iota(jnp.int32, shape, dim)


def one_hot(hit):
    return jnp.where(hit, 1.0, 0.0).astype(BF)


def params():
    return pltpu.CompilerParams(vmem_limit_bytes=VMEM_BYTES)


def cost(mflops, kbytes):
    return pl.CostEstimate(
        flops=int(mflops * 1e6), bytes_accessed=int(kbytes * 1024), transcendentals=0
    )


def pick_kernel(send_ref, *refs):
    count = len(refs) - 3
    sources = refs[:count]
    left_ref, right_ref, hot_ref = refs[count:]
    rows = sources[0].shape[0]
    capacity = send_ref.shape[1]

    @pl.when(pl.program_id(0) == 0)
    def _():
        lane = iota((capacity, rows), 1)
        for side in range(2):
            named = along_rows(send_ref[side : side + 1, :], 128)
            for start in range(0, rows, 128):
                hot_ref[side * capacity : (side + 1) * capacity, start : start + 128] = one_hot(
                    named == lane[:, :128] + start
                )

    for index, source in enumerate(sources):
        picked = dot(hot_ref[...], source[...]).astype(BF)
        left_ref[index] = picked[:capacity]
        right_ref[index] = picked[capacity:]


def pick(send, arrays, cols):
    rows, features = arrays[0].shape
    capacity = send.shape[1]
    count = len(arrays)
    block = pl.BlockSpec((rows, cols), lambda g: (0, g))
    out = pl.BlockSpec((count, capacity, cols), lambda g: (0, 0, g))
    shape = jax.ShapeDtypeStruct((count, capacity, features), BF)
    return pl.pallas_call(
        pick_kernel,
        grid=(features // cols,),
        in_specs=[pl.BlockSpec((2, capacity), lambda g: (0, 0))] + [block] * count,
        out_specs=[out, out],
        out_shape=[shape, shape],
        scratch_shapes=[pltpu.VMEM((2 * capacity, rows), BF)],
        compiler_params=params(),
        cost_estimate=cost(268 * count, 1536 * count),
        name="pick",
    )(send, *arrays)


def prep_kernel(
    docs_ref, first_ref, take_ref, log_ref, q_ref, k_ref, v_ref,
    qo_ref, ko_ref, vo_ref, hot_ref, weight_ref, cols_ref, through_ref,
    own_ref, mask_ref, rows_ref,
):
    rows = q_ref.shape[0]
    heads = log_ref.shape[1]
    capacity = hot_ref.shape[1] // 2
    step = pl.program_id(0)
    half = rows // 2

    @pl.when(step == 0)
    def _():
        first = first_ref[0]
        position = first + iota((rows, 1), 0)
        position_row = first + iota((1, rows), 1)
        segment = jnp.zeros((rows, 1), jnp.int32)
        segment_row = jnp.zeros((1, rows), jnp.int32)
        segment_first = jnp.int32(0)
        segment_last = jnp.int32(0)
        opens_first = jnp.int32(0)
        opens = jnp.int32(0)
        start = jnp.int32(0)
        for n in range(docs_ref.shape[0]):
            segment += (position >= start).astype(jnp.int32)
            segment_row += (position_row >= start).astype(jnp.int32)
            segment_first += (first >= start).astype(jnp.int32)
            segment_last += (first + rows - 1 >= start).astype(jnp.int32)
            opens_first += (first == start).astype(jnp.int32)
            opens += ((start >= first) & (start < first + rows)).astype(jnp.int32)
            start += docs_ref[n]
        below = iota((rows, rows), 0) >= iota((rows, rows), 1)
        scale = -0.5 * math.log2(q_ref.shape[1] // 2)
        mask_ref[...] = jnp.where((segment == segment_row) & below, scale, MASKED)
        triangle = one_hot(below)
        logs = jnp.concatenate([log_ref[...], jnp.zeros((rows, 128 - heads), F32)], axis=1)
        high = logs.astype(BF)
        rest = logs - high.astype(F32)
        middle = rest.astype(BF)
        low = (rest - middle.astype(F32)).astype(BF)
        running = (dot(triangle, high) + (dot(triangle, middle) + dot(triangle, low))) * LOG2E
        turned = running.T
        final = running[rows - 1 : rows, :]
        keep_f = segment == segment_last
        keep_e = (segment == segment_first) & (opens_first == 0)
        leaving = jnp.where(keep_f, jnp.exp2(final - running), 0.0)
        entering = jnp.where(keep_e, jnp.exp2(running + scale), 0.0)
        through = jnp.where(opens == 0, jnp.exp2(final), 0.0)
        t_high = through.astype(BF).astype(F32)
        t_middle = (through - t_high).astype(BF).astype(F32)
        t_low = through - t_high - t_middle
        line = iota((16, 128), 0)
        for h in range(heads):
            g, t = h // 2, h % 2
            cols_ref[g, :, t : t + 1] = leaving[:, h : h + 1]
            cols_ref[g, :, 2 + t : 3 + t] = entering[:, h : h + 1]
            cols_ref[g, :, 4 + t : 5 + t] = running[:, h : h + 1]
            rows_ref[g, t : t + 1, :] = turned[h : h + 1, :]
            parts = [
                jnp.broadcast_to(x[:, h : h + 1], (16, 128)) for x in (t_high, t_middle, t_low)
            ]
            through_ref[h] = jnp.where(
                line == 0,
                parts[0],
                jnp.where(line == 1, parts[1], jnp.where(line == 2, parts[2], 0.0)),
            ).astype(BF)
        lane = iota((rows, 128), 1)
        taken = along_rows(take_ref[...], 128)
        for start_row in range(0, rows, 128):
            own_ref[:, start_row : start_row + 128] = one_hot(
                taken - capacity == lane + start_row
            )
        hot_ref[:, :capacity] = one_hot(taken == lane)
        hot_ref[:, capacity:] = one_hot(taken - (capacity + rows) == lane)

    own = own_ref[...]
    qo_ref[...] = dot(own, q_ref[...]).astype(BF)
    ko_ref[...] = dot(own, k_ref[...]).astype(BF)
    vo_ref[...] = dot(own, v_ref[...]).astype(BF)
    for t in range(2):
        column = cols_ref[step, :, 4 + t : 5 + t]
        row = rows_ref[step, t : t + 1, :]
        for i in range(2):
            top, width = i * half, (i + 1) * half
            weight_ref[t, top : top + half, :width] = jnp.exp2(
                (column[top : top + half] - row[:, :width])
                + mask_ref[top : top + half, :width]
            )


def prep(docs, first, take, log_decay, q, k, v, capacity):
    rows, features = q.shape
    heads = log_decay.shape[1]
    pairs = heads // 2
    cols = features // pairs
    smem = pl.BlockSpec(memory_space=pltpu.SMEM)
    block = pl.BlockSpec((rows, cols), lambda g: (0, g))
    whole2 = lambda a, b: pl.BlockSpec((a, b), lambda g: (0, 0))
    whole3 = lambda a, b, c: pl.BlockSpec((a, b, c), lambda g: (0, 0, 0))
    own = jax.ShapeDtypeStruct((rows, features), BF)
    return pl.pallas_call(
        prep_kernel,
        grid=(pairs,),
        in_specs=[smem, smem, whole2(1, rows), whole2(rows, heads), block, block, block],
        out_specs=[
            block, block, block,
            whole2(rows, 2 * capacity),
            pl.BlockSpec((2, rows, rows), lambda g: (g, 0, 0)),
            whole3(pairs, rows, 8),
            whole3(heads, 16, 128),
        ],
        out_shape=[
            own, own, own,
            jax.ShapeDtypeStruct((rows, 2 * capacity), BF),
            jax.ShapeDtypeStruct((heads, rows, rows), F32),
            jax.ShapeDtypeStruct((pairs, rows, 8), F32),
            jax.ShapeDtypeStruct((heads, 16, 128), BF),
        ],
        scratch_shapes=[
            pltpu.VMEM((rows, rows), BF),
            pltpu.VMEM((rows, rows), F32),
            pltpu.VMEM((pairs, 8, rows), F32),
        ],
        compiler_params=params(),
        cost_estimate=cost(6000, 16000),
        name="prep",
    )(docs, first, take, log_decay, q, k, v)


def arrived(own_ref, hot_ref, left, right):
    extra = dot(hot_ref[...], jnp.concatenate([left, right], axis=0))
    return own_ref[...] + extra.astype(BF)


def state_kernel(hot_ref, ko_ref, vo_ref, left_ref, right_ref, cols_ref, through_ref, k_ref, v_ref, s_ref):
    dk = s_ref.shape[2]
    k = arrived(ko_ref, hot_ref, left_ref[0], right_ref[0])
    v = arrived(vo_ref, hot_ref, left_ref[1], right_ref[1])
    k_ref[...] = k
    v_ref[...] = v
    for t in range(2):
        part = slice(t * dk, (t + 1) * dk)
        kf = (k[:, part].astype(F32) * cols_ref[0, :, t : t + 1]).astype(BF)
        s_ref[t, :dk, :] = dot_tn(kf, v[:, part]).astype(BF)
        s_ref[t, dk:, :] = through_ref[t]


def state(hot, k_own, v_own, left, right, cols, through):
    rows, features = k_own.shape
    pairs = cols.shape[0]
    heads = 2 * pairs
    width = features // pairs
    dk = width // 2
    capacity = left.shape[1]
    block = pl.BlockSpec((rows, width), lambda g: (0, g))
    side = pl.BlockSpec((2, capacity, width), lambda g: (0, 0, g))
    full = jax.ShapeDtypeStruct((rows, features), BF)
    return pl.pallas_call(
        state_kernel,
        grid=(pairs,),
        in_specs=[
            pl.BlockSpec((rows, 2 * capacity), lambda g: (0, 0)),
            block, block, side, side,
            pl.BlockSpec((1, rows, 8), lambda g: (g, 0, 0)),
            pl.BlockSpec((2, 16, 128), lambda g: (g, 0, 0)),
        ],
        out_specs=[block, block, pl.BlockSpec((2, dk + 16, dk), lambda g: (g, 0, 0))],
        out_shape=[full, full, jax.ShapeDtypeStruct((heads, dk + 16, dk), BF)],
        compiler_params=params(),
        cost_estimate=cost(2000, 6000),
        name="state",
    )(hot, k_own, v_own, left, right, cols, through)


def inside_kernel(hot_ref, qo_ref, left_ref, right_ref, k_ref, v_ref, weight_ref, q_ref, p_ref, o_ref):
    rows, width = k_ref.shape
    dk, half = width // 2, rows // 2
    q = arrived(qo_ref, hot_ref, left_ref[0], right_ref[0])
    q_ref[...] = q
    for t in range(2):
        part = slice(t * dk, (t + 1) * dk)
        for i in range(2):
            top, reach = i * half, (i + 1) * half
            scores = dot_nt(q[top : top + half, part], k_ref[:reach, part])
            p = (scores * weight_ref[t, top : top + half, :reach]).astype(BF)
            p_ref[t, top : top + half, :reach] = p
            o_ref[top : top + half, part] = dot(p, v_ref[:reach, part])


def inside(hot, q_own, left, right, k, v, weight):
    rows, features = k.shape
    heads = weight.shape[0]
    pairs = heads // 2
    width = features // pairs
    capacity = left.shape[1]
    block = pl.BlockSpec((rows, width), lambda g: (0, g))
    side = pl.BlockSpec((1, capacity, width), lambda g: (0, 0, g))
    square = pl.BlockSpec((2, rows, rows), lambda g: (g, 0, 0))
    return pl.pallas_call(
        inside_kernel,
        grid=(pairs,),
        in_specs=[
            pl.BlockSpec((rows, 2 * capacity), lambda g: (0, 0)),
            block, side, side, block, block, square,
        ],
        out_specs=[block, square, block],
        out_shape=[
            jax.ShapeDtypeStruct((rows, features), BF),
            jax.ShapeDtypeStruct((heads, rows, rows), BF),
            jax.ShapeDtypeStruct((rows, features), F32),
        ],
        compiler_params=params(),
        cost_estimate=cost(3000, 18000),
        name="inside",
    )(hot, q_own, left, right, k, v, weight)


def joined(near_ref, far_ref, t, dk):
    through = jnp.sum(near_ref[t, dk:, :].astype(F32), axis=0, keepdims=True)
    near = near_ref[t, :dk, :].astype(F32)
    return (near + through * far_ref[t, :dk, :].astype(F32)).astype(BF)


def output_kernel(scale_ref, o_ref, q_ref, near_ref, far_ref, cols_ref, ct_ref, u_ref, h_ref, sums_ref, sq_ref, cross_ref):
    dk = q_ref.shape[1] // 2
    step = pl.program_id(0)

    @pl.when(step == 0)
    def _():
        sq_ref[...] = jnp.zeros_like(sq_ref)
        cross_ref[...] = jnp.zeros_like(cross_ref)

    squares, cross = sq_ref[...], cross_ref[...]
    for t in range(2):
        part = slice(t * dk, (t + 1) * dk)
        h = joined(near_ref, far_ref, t, dk)
        h_ref[t] = h
        outer = dot(q_ref[:, part], h) * cols_ref[0, :, 2 + t : 3 + t]
        u = (o_ref[:, part] + outer) * scale_ref[2 * step + t]
        u_ref[:, part] = u
        squares += u * u
        cross += ct_ref[:, part].astype(F32) * u
    sq_ref[...] = squares
    cross_ref[...] = cross

    @pl.when(step == pl.num_programs(0) - 1)
    def _():
        sums_ref[0:1, :] = jnp.sum(squares.T, axis=0, keepdims=True)
        sums_ref[1:2, :] = jnp.sum(cross.T, axis=0, keepdims=True)


def output(head_scale, o, q, near, far, cols, ct):
    rows, features = q.shape
    pairs = cols.shape[0]
    width = features // pairs
    dk = width // 2
    block = pl.BlockSpec((rows, width), lambda g: (0, g))
    message = pl.BlockSpec((2, dk + 16, dk), lambda g: (g, 0, 0))
    return pl.pallas_call(
        output_kernel,
        grid=(pairs,),
        in_specs=[
            pl.BlockSpec(memory_space=pltpu.SMEM),
            block, block, message, message,
            pl.BlockSpec((1, rows, 8), lambda g: (g, 0, 0)),
            block,
        ],
        out_specs=[
            block,
            pl.BlockSpec((2, dk, dk), lambda g: (g, 0, 0)),
            pl.BlockSpec((2, rows), lambda g: (0, 0)),
        ],
        out_shape=[
            jax.ShapeDtypeStruct((rows, features), F32),
            jax.ShapeDtypeStruct((2 * pairs, dk, dk), BF),
            jax.ShapeDtypeStruct((2, rows), F32),
        ],
        scratch_shapes=[pltpu.VMEM((rows, dk), F32), pltpu.VMEM((rows, dk), F32)],
        compiler_params=params(),
        cost_estimate=cost(400, 8000),
        name="output",
    )(head_scale, o, q, near, far, cols, ct)


def norm_kernel(total, scale_ref, sums_ref, u_ref, ct_ref, q_ref, cols_ref, through_ref, n_ref, g_ref, s_ref, inv_ref, mean_ref):
    dk = q_ref.shape[1] // 2
    step = pl.program_id(0)

    @pl.when(step == 0)
    def _():
        inverse = lax.rsqrt(along_rows(sums_ref[0:1, :], dk) / total + EPSILON)
        inv_ref[...] = inverse
        mean_ref[...] = inverse * inverse * inverse * (along_rows(sums_ref[1:2, :], dk) / total)

    inverse, mean = inv_ref[...], mean_ref[...]
    for t in range(2):
        part = slice(t * dk, (t + 1) * dk)
        u = u_ref[:, part]
        n_ref[:, part] = (u * inverse).astype(BF)
        g = ((inverse * ct_ref[:, part].astype(F32) - u * mean) * scale_ref[2 * step + t]).astype(BF)
        g_ref[:, part] = g
        qe = (q_ref[:, part].astype(F32) * cols_ref[0, :, 2 + t : 3 + t]).astype(BF)
        s_ref[t, :dk, :] = dot_tn(qe, g).astype(BF)
        s_ref[t, dk:, :] = through_ref[t]


def norm(total, head_scale, sums, u, ct, q, cols, through):
    rows, features = q.shape
    pairs = cols.shape[0]
    width = features // pairs
    dk = width // 2
    block = pl.BlockSpec((rows, width), lambda g: (0, g))
    full = jax.ShapeDtypeStruct((rows, features), BF)
    return pl.pallas_call(
        functools.partial(norm_kernel, total),
        grid=(pairs,),
        in_specs=[
            pl.BlockSpec(memory_space=pltpu.SMEM),
            pl.BlockSpec((2, rows), lambda g: (0, 0)),
            block, block, block,
            pl.BlockSpec((1, rows, 8), lambda g: (g, 0, 0)),
            pl.BlockSpec((2, 16, 128), lambda g: (g, 0, 0)),
        ],
        out_specs=[block, block, pl.BlockSpec((2, dk + 16, dk), lambda g: (g, 0, 0))],
        out_shape=[full, full, jax.ShapeDtypeStruct((2 * pairs, dk + 16, dk), BF)],
        scratch_shapes=[pltpu.VMEM((rows, dk), F32), pltpu.VMEM((rows, dk), F32)],
        compiler_params=params(),
        cost_estimate=cost(400, 8000),
        name="norm",
    )(head_scale, sums, u, ct, q, cols, through)


def slots_hot(take_ref, hot_ref, capacity, rows):
    taken = jnp.broadcast_to(take_ref[...], (capacity, rows))
    slot = iota((capacity, rows), 0)
    hot_ref[:capacity, :] = one_hot(taken == slot)
    hot_ref[capacity:, :] = one_hot(taken - (capacity + rows) == slot)


def grad_q_kernel(take_ref, g_ref, k_ref, v_ref, h_ref, weight_ref, cols_ref, dq_ref, z_ref, left_ref, right_ref, hot_ref):
    rows, width = k_ref.shape
    dk, half = width // 2, rows // 2
    capacity = left_ref.shape[1]

    @pl.when(pl.program_id(0) == 0)
    def _():
        slots_hot(take_ref, hot_ref, capacity, rows)

    for t in range(2):
        part = slice(t * dk, (t + 1) * dk)
        for i in range(2):
            top, reach = i * half, (i + 1) * half
            g = g_ref[top : top + half, part]
            scores = dot_nt(g, v_ref[:reach, part])
            z = (scores * weight_ref[t, top : top + half, :reach]).astype(BF)
            z_ref[t, top : top + half, :reach] = z
            outer = dot_nt(g, h_ref[t]) * cols_ref[0, top : top + half, 2 + t : 3 + t]
            dq_ref[top : top + half, part] = (dot(z, k_ref[:reach, part]) + outer).astype(BF)
    back = dot(hot_ref[...], dq_ref[...]).astype(BF)
    left_ref[0] = back[:capacity]
    right_ref[0] = back[capacity:]


def grad_q(take, g, k, v, h, weight, cols, capacity):
    rows, features = k.shape
    pairs = cols.shape[0]
    width = features // pairs
    dk = width // 2
    block = pl.BlockSpec((rows, width), lambda g: (0, g))
    side = pl.BlockSpec((1, capacity, width), lambda g: (0, 0, g))
    square = pl.BlockSpec((2, rows, rows), lambda g: (g, 0, 0))
    return pl.pallas_call(
        grad_q_kernel,
        grid=(pairs,),
        in_specs=[
            pl.BlockSpec((1, rows), lambda g: (0, 0)),
            block, block, block,
            pl.BlockSpec((2, dk, dk), lambda g: (g, 0, 0)),
            square,
            pl.BlockSpec((1, rows, 8), lambda g: (g, 0, 0)),
        ],
        out_specs=[block, square, side, side],
        out_shape=[
            jax.ShapeDtypeStruct((rows, features), BF),
            jax.ShapeDtypeStruct((2 * pairs, rows, rows), BF),
            jax.ShapeDtypeStruct((1, capacity, features), BF),
            jax.ShapeDtypeStruct((1, capacity, features), BF),
        ],
        scratch_shapes=[pltpu.VMEM((2 * capacity, rows), BF)],
        compiler_params=params(),
        cost_estimate=cost(3000, 18000),
        name="grad_q",
    )(take, g, k, v, h, weight, cols)


def inner_kernel(z_ref, p_ref, q_ref, g_ref, dk_ref, dv_ref):
    rows, width = q_ref.shape
    dk, half = width // 2, rows // 2
    for t in range(2):
        part = slice(t * dk, (t + 1) * dk)
        for square, source, target in ((z_ref, q_ref, dk_ref), (p_ref, g_ref, dv_ref)):
            for j in range(2):
                top = j * half
                target[top : top + half, part] = dot_tn(
                    square[t, top:, top : top + half], source[top:, part]
                )


def inner(z, p, q, g):
    rows, features = q.shape
    heads = z.shape[0]
    pairs = heads // 2
    block = pl.BlockSpec((rows, features // pairs), lambda g: (0, g))
    square = pl.BlockSpec((2, rows, rows), lambda g: (g, 0, 0))
    full = jax.ShapeDtypeStruct((rows, features), F32)
    return pl.pallas_call(
        inner_kernel,
        grid=(pairs,),
        in_specs=[square, square, block, block],
        out_specs=[block, block],
        out_shape=[full, full],
        compiler_params=params(),
        cost_estimate=cost(3000, 14000),
        name="inner",
    )(z, p, q, g)


def grad_kv_kernel(take_ref, near_ref, far_ref, k_ref, v_ref, cols_ref, dki_ref, dvi_ref, dk_ref, dv_ref, left_ref, right_ref, hot_ref):
    rows, width = k_ref.shape
    dk = width // 2
    capacity = left_ref.shape[1]

    @pl.when(pl.program_id(0) == 0)
    def _():
        slots_hot(take_ref, hot_ref, capacity, rows)

    for t in range(2):
        part = slice(t * dk, (t + 1) * dk)
        state_grad = joined(near_ref, far_ref, t, dk)
        leaving = cols_ref[0, :, t : t + 1]
        dk_ref[:, part] = (dki_ref[:, part] + leaving * dot_nt(v_ref[:, part], state_grad)).astype(BF)
        dv_ref[:, part] = (dvi_ref[:, part] + leaving * dot(k_ref[:, part], state_grad)).astype(BF)
    for index, source in enumerate((dk_ref, dv_ref)):
        back = dot(hot_ref[...], source[...]).astype(BF)
        left_ref[index] = back[:capacity]
        right_ref[index] = back[capacity:]


def grad_kv(take, near, far, k, v, cols, dk_inner, dv_inner, capacity):
    rows, features = k.shape
    pairs = cols.shape[0]
    width = features // pairs
    dk = width // 2
    block = pl.BlockSpec((rows, width), lambda g: (0, g))
    side = pl.BlockSpec((2, capacity, width), lambda g: (0, 0, g))
    message = pl.BlockSpec((2, dk + 16, dk), lambda g: (g, 0, 0))
    full = jax.ShapeDtypeStruct((rows, features), BF)
    return pl.pallas_call(
        grad_kv_kernel,
        grid=(pairs,),
        in_specs=[
            pl.BlockSpec((1, rows), lambda g: (0, 0)),
            message, message, block, block,
            pl.BlockSpec((1, rows, 8), lambda g: (g, 0, 0)),
            block, block,
        ],
        out_specs=[block, block, side, side],
        out_shape=[
            full, full,
            jax.ShapeDtypeStruct((2, capacity, features), BF),
            jax.ShapeDtypeStruct((2, capacity, features), BF),
        ],
        scratch_shapes=[pltpu.VMEM((2 * capacity, rows), BF)],
        compiler_params=params(),
        cost_estimate=cost(1000, 10000),
        name="grad_kv",
    )(take, near, far, k, v, cols, dk_inner, dv_inner)


def own_kernel(capacity, take_ref, *refs):
    count = (len(refs) - 1) // 2
    hot_ref = refs[-1]
    rows = refs[0].shape[0]

    @pl.when(pl.program_id(0) == 0)
    def _():
        taken = jnp.broadcast_to(take_ref[...], (rows, rows))
        hot_ref[...] = one_hot(taken - capacity == iota((rows, rows), 0))

    for source, target in zip(refs[:count], refs[count : 2 * count]):
        target[...] = dot(hot_ref[...], source[...]).astype(BF)


def own(take, arrays, capacity, cols):
    rows, features = arrays[0].shape
    count = len(arrays)
    block = pl.BlockSpec((rows, cols), lambda g: (0, g))
    full = jax.ShapeDtypeStruct((rows, features), BF)
    return pl.pallas_call(
        functools.partial(own_kernel, capacity),
        grid=(features // cols,),
        in_specs=[pl.BlockSpec((1, rows), lambda g: (0, 0))] + [block] * count,
        out_specs=[block] * count,
        out_shape=[full] * count,
        scratch_shapes=[pltpu.VMEM((rows, rows), BF)],
        compiler_params=params(),
        cost_estimate=cost(540 * count, 2048 * count),
        name="own",
    )(take, *arrays)


def finish_kernel(send_ref, left_ref, right_ref, *refs):
    count = (len(refs) - 1) // 2
    hot_ref = refs[-1]
    rows = refs[0].shape[0]
    capacity = send_ref.shape[1]

    @pl.when(pl.program_id(0) == 0)
    def _():
        line = iota((rows, capacity), 0)
        for side in range(2):
            named = jnp.broadcast_to(send_ref[side : side + 1, :], (rows, capacity))
            hot_ref[:, side * capacity : (side + 1) * capacity] = one_hot(named == line)

    for index in range(count):
        back = jnp.concatenate([left_ref[index], right_ref[index]], axis=0)
        refs[count + index][...] = refs[index][...] + dot(hot_ref[...], back).astype(BF)


def finish(send, left, right, arrays, cols):
    rows, features = arrays[0].shape
    count = len(arrays)
    capacity = send.shape[1]
    block = pl.BlockSpec((rows, cols), lambda g: (0, g))
    side = pl.BlockSpec((count, capacity, cols), lambda g: (0, 0, g))
    full = jax.ShapeDtypeStruct((rows, features), BF)
    return pl.pallas_call(
        finish_kernel,
        grid=(features // cols,),
        in_specs=[pl.BlockSpec((2, capacity), lambda g: (0, 0)), side, side] + [block] * count,
        out_specs=[block] * count,
        out_shape=[full] * count,
        scratch_shapes=[pltpu.VMEM((rows, 2 * capacity), BF)],
        compiler_params=params(),
        cost_estimate=cost(270 * count, 3000 * count),
        name="finish",
    )(send, left, right, *arrays)


def shifted(array, by):
    peers = lax.axis_size("seq")
    return lax.ppermute(
        array, "seq", [(i, i + by) for i in range(peers) if 0 <= i + by < peers]
    )


def carried(message, direction):
    reach = lax.axis_size("seq") // 4
    if reach <= 2:
        return shifted(message, direction), shifted(message, 2 * direction)
    size = message.shape[2]
    own_state = message[:, :size].astype(F32)
    through = jnp.sum(message[:, size:, :1].astype(F32), axis=1, keepdims=True)

    def relay(_, state_here):
        return shifted((through * state_here + own_state).astype(BF), direction).astype(F32)

    incoming = lax.fori_loop(0, reach, relay, jnp.zeros_like(own_state)).astype(BF)
    near = jnp.concatenate([incoming, jnp.zeros_like(message[:, size:])], axis=1)
    return near, jnp.zeros_like(message)


def on_device(
    queries, key_vectors, value_vectors, log_decay, head_scale,
    send_rows, take_rows, doc_lengths, cotangent,
):
    rows, features = queries.shape
    heads = head_scale.shape[0]
    capacity = send_rows.shape[2]
    cols = 2 * (features // heads)
    send = send_rows.reshape(2, capacity)
    take = take_rows.reshape(1, rows)
    first = (lax.axis_index("seq") * rows).astype(jnp.int32).reshape(1)
    total = features * lax.axis_size("head")

    kv_left, kv_right = pick(send, (key_vectors, value_vectors), cols)
    q_left, q_right = pick(send, (queries,), cols)
    kv_before, kv_after = shifted(kv_right, 1), shifted(kv_left, -1)
    q_before, q_after = shifted(q_right, 1), shifted(q_left, -1)
    q_own, k_own, v_own, hot, weight, columns, through = prep(
        doc_lengths, first, take, log_decay, queries, key_vectors, value_vectors, capacity
    )
    k, v, message = state(hot, k_own, v_own, kv_before, kv_after, columns, through)
    near, far = carried(message, 1)
    q, probs, o_inside = inside(hot, q_own, q_before, q_after, k, v, weight)
    u, state_low, sums = output(head_scale, o_inside, q, near, far, columns, cotangent)
    sums = lax.psum(sums, "head")
    normed, g, grad_message = norm(total, head_scale, sums, u, cotangent, q, columns, through)
    grad_near, grad_far = carried(grad_message, -1)
    dq, z, dq_left, dq_right = grad_q(take, g, k, v, state_low, weight, columns, capacity)
    dq_before, dq_after = shifted(dq_right, 1), shifted(dq_left, -1)
    dk_inner, dv_inner = inner(z, probs, q, g)
    dk, dv, kv_left, kv_right = grad_kv(
        take, grad_near, grad_far, k, v, columns, dk_inner, dv_inner, capacity
    )
    dkv_before, dkv_after = shifted(kv_right, 1), shifted(kv_left, -1)
    dq_own, dk_own, dv_own = own(take, (dq, dk, dv), capacity, cols)
    (grad_queries,) = finish(send, dq_before, dq_after, (dq_own,), cols)
    grad_keys, grad_values = finish(send, dkv_before, dkv_after, (dk_own, dv_own), cols)
    return normed, grad_queries, grad_keys, grad_values


def solution(mesh):
    both = P("seq", "head")
    in_specs = (both, both, both, both, P("head"), P("seq", None, None), P("seq"), P(), both)
    return jax.shard_map(
        on_device, mesh=mesh, in_specs=in_specs, out_specs=(both,) * 4, check_vma=False
    )
```

profile of v0, /device:TPU:0, one launch (start us, length us, event | category | flops | bytes accessed | tf_op | source)
XLA Modules:
  0.0 145.7 jit_solution(1988789949169061063)
XLA Ops:
  2.6 2.2 %pick.2 = (bf16[1,128,1024]{2,1,0:T(8,128)(2,1)}, bf16[1,128,1024]{2,1,0:T(8,128)(2,1)}) custom-call(s32[2,128]{1,0:T(2,128)S(1)} %bitcast.3, bf16[512,1024]{1,0:T(8,128)(2,1)S(1)} %copy-done.7), custom_call_target="tpu_custom_call" | custom-call | flops 268000000 | bytes 1572864 | tf_op jit(solution)/shard_map/pick/pallas_call | solution.py:85
  4.8 4.9 %collective-permute-start = (bf16[1,128,1024]{2,1,0:T(8,128)(2,1)}, bf16[1,128,1024]{2,1,0:T(8,128)(2,1)S(1)}, u32[]{:S(2)}, u32[]{:S(2)}) collective-permute-start(bf16[1,128,1024]{2,1,0:T(8,128)(2,1)} %get-tuple-element.44), channel_id=1, source_target_pairs={{0,4},{4,8},{8,12},{12,16},{16,20},{20,24},{24,28},{1,5},{5,9},{9,... | collective-permute-start | bytes 786440 | tf_op jit(solution)/shard_map/ppermute | solution.py:649
  9.7 1.3 collective-permute-start.1
  14.1 2.6 %pick.3 = (bf16[2,128,1024]{2,1,0:T(8,128)(2,1)}, bf16[2,128,1024]{2,1,0:T(8,128)(2,1)}) custom-call(s32[2,128]{1,0:T(2,128)S(1)} %bitcast.4, bf16[512,1024]{1,0:T(8,128)(2,1)S(1)} %copy-done.9, bf16[512,1024]{1,0:T(8,128)(2,1)S(1)} %copy-done.11), custom_call_target="tpu_custom_call" | custom-call | flops 536000000 | bytes 3145728 | tf_op jit(solution)/shard_map/pick/pallas_call | solution.py:85
  16.7 5.4 %collective-permute-start.2 = (bf16[2,128,1024]{2,1,0:T(8,128)(2,1)}, bf16[2,128,1024]{2,1,0:T(8,128)(2,1)}, u32[]{:S(2)}, u32[]{:S(2)}) collective-permute-start(bf16[2,128,1024]{2,1,0:T(8,128)(2,1)} %get-tuple-element.48), channel_id=1, source_target_pairs={{0,4},{4,8},{8,12},{12,16},{16,20},{20,24},{24,28},{1,5},{5,9},{9,... | collective-permute-start | bytes 1572872 | tf_op jit(solution)/shard_map/ppermute | solution.py:649
  22.1 1.3 collective-permute-start.3
  26.4 7.5 %prep.1 = (bf16[512,1024]{1,0:T(8,128)(2,1)S(1)}, bf16[512,1024]{1,0:T(8,128)(2,1)S(1)}, bf16[512,1024]{1,0:T(8,128)(2,1)S(1)}, bf16[512,256]{1,0:T(8,128)(2,1)S...) custom-call(s32[8]{0:T(128)S(1)} %copy-done.20, s32[1]{0:T(128)} %bitcast.first_ref, ...), custom_call_target="tpu_custom_call" | custom-call | flops 6000000000 | bytes 16384000 | tf_op jit(solution)/shard_map/prep/pallas_call | solution.py:198
  34.0 9.6 %collective-permute-done.2.left_ref = bf16[2,128,1024]{2,1,0:T(8,128)(2,1)} collective-permute-done((bf16[2,128,1024]{2,1,0:T(8,128)(2,1)}, bf16[2,128,1024]{2,1,0:T(8,128)(2,1)}, u32[]{:S(2)}, u32[]{:S(2)}) %collective-permute-start.2) | collective-permute-done | bytes 524320 | tf_op jit(solution)/shard_map/ppermute | solution.py:649
  43.6 4.0 %state.1 = (bf16[512,1024]{1,0:T(8,128)(2,1)S(1)}, bf16[512,1024]{1,0:T(8,128)(2,1)S(1)}, bf16[8,144,128]{2,1,0:T(8,128)(2,1)S(1)}) custom-call(bf16[512,256]{1,0:T(8,128)(2,1)S(1)} %get-tuple-element.42.hot_ref, bf16[512,1024]{1,0:T(8,128)(2,1)S(1)} %get-tuple-element.46.ko_ref, bf16[512,1024]{1,0:T(8,128)(2,1)S(1)} %get-tuple-element.47.vo_ref, ...), custom_call_target="tpu_custom_call" | custom-call | flops 2000000000 | bytes 6144000 | tf_op jit(solution)/shard_map/state/pallas_call | solution.py:255
  47.7 6.1 %collective-permute-start.5 = (bf16[8,144,128]{2,1,0:T(8,128)(2,1)S(1)}, bf16[8,144,128]{2,1,0:T(8,128)(2,1)S(1)}, u32[]{:S(2)}, u32[]{:S(2)}) collective-permute-start(bf16[8,144,128]{2,1,0:T(8,128)(2,1)S(1)} %get-tuple-element.57), channel_id=1, source_target_pairs={{0,8},{4,12},{8,16},{12,20},{16,24},{20,28},{1,9},{5,13},{9,17},{1... | collective-permute-start | bytes 884744 | tf_op jit(solution)/shard_map/ppermute | solution.py:649
  53.8 1.8 %collective-permute-start.4 = (bf16[8,144,128]{2,1,0:T(8,128)(2,1)S(1)}, bf16[8,144,128]{2,1,0:T(8,128)(2,1)S(1)}, u32[]{:S(2)}, u32[]{:S(2)}) collective-permute-start(bf16[8,144,128]{2,1,0:T(8,128)(2,1)S(1)} %get-tuple-element.57), channel_id=1, source_target_pairs={{0,4},{4,8},{8,12},{12,16},{16,20},{20,24},{24,28},{1,5},{5,9},{9,... | collective-permute-start | bytes 884744 | tf_op jit(solution)/shard_map/ppermute | solution.py:649
  55.6 6.8 %inside.1 = (bf16[512,1024]{1,0:T(8,128)(2,1)S(1)}, bf16[8,512,512]{2,1,0:T(8,128)(2,1)S(1)}, f32[512,1024]{1,0:T(8,128)S(1)}) custom-call(bf16[512,256]{1,0:T(8,128)(2,1)S(1)} %get-tuple-element.42.hot_ref, bf16[512,1024]{1,0:T(8,128)(2,1)S(1)} %get-tuple-element.43.qo_ref, bf16[1,128,1024]{2,1,0:T(8,128)(2,1)S(1)} %collective-permute-done.left_ref, ...), custom_call_target="tpu_custom_call" | custom-call | flops 3000000000 | bytes 18432000 | tf_op jit(solution)/shard_map/inside/pallas_call | solution.py:296
  62.4 2.0 %copy-done.19 = bf16[8,512,512]{2,1,0:T(8,128)(2,1)} copy-done((bf16[8,512,512]{2,1,0:T(8,128)(2,1)}, bf16[8,512,512]{2,1,0:T(8,128)(2,1)S(1)}, u32[]{:S(2)}) %copy-start.19) | copy-done | bytes 4194328
  64.5 2.7 %output.1 = (f32[512,1024]{1,0:T(8,128)S(1)}, bf16[8,128,128]{2,1,0:T(8,128)(2,1)S(1)}, f32[2,512]{1,0:T(2,128)S(1)}) custom-call(f32[8]{0:T(128)S(1)} %copy-done.18, f32[512,1024]{1,0:T(8,128)S(1)} %get-tuple-element.55.o_ref, bf16[512,1024]{1,0:T(8,128)(2,1)S(1)} %get-tuple-element.56.q_ref, bf16[8,144,128]{2,1,0:T(8,128)(2,1)S(1)} %collective-permute-done.4.near_ref, ...), custom_call_target="tpu_custom_call" | custom-call | flops 400000000 | bytes 8192000 | tf_op jit(solution)/shard_map/output/pallas_call | solution.py:356
  67.2 1.3 copy-done.5
  68.5 5.9 %psum.7.sums_ref = f32[2,512]{1,0:T(2,128)S(1)} all-reduce(f32[2,512]{1,0:T(2,128)S(1)} %get-tuple-element.58), channel_id=1, replica_groups=mesh['seq'=8,'head'=4] {'head'}, use_global_device_ids=true, to_apply=%region_0.0 | all-reduce | flops 1024 | bytes 8192 | tf_op jit(solution)/shard_map/psum | solution.py:694
  74.4 1.2 copy-done.1
  76.8 1.6 %copy-done.6 = f32[512,1024]{1,0:T(8,128)S(1)} copy-done((f32[512,1024]{1,0:T(8,128)S(1)}, f32[512,1024]{1,0:T(8,128)}, u32[]{:S(2)}) %copy-start.6) | copy-done | bytes 2097176
  78.4 3.8 %norm.1 = (bf16[512,1024]{1,0:T(8,128)(2,1)}, bf16[512,1024]{1,0:T(8,128)(2,1)S(1)}, bf16[8,144,128]{2,1,0:T(8,128)(2,1)S(1)}) custom-call(f32[8]{0:T(128)S(1)} %copy-done.18, f32[2,512]{1,0:T(2,128)S(1)} %psum.7.sums_ref, f32[512,1024]{1,0:T(8,128)S(1)} %copy-done.6, bf16[512,1024]{1,0:T(8,128)(2,1)S(1)} %copy-done.1, bf16[512,1024]{1,0:T(8,128)(2,1)S(1)} %copy-done.3, ...), custom_call_target="tpu_custom_call" | custom-call | flops 400000000 | bytes 8192000 | tf_op jit(solution)/shard_map/norm/pallas_call | solution.py:411
  82.2 1.3 collective-permute-start.9
  83.5 1.3 collective-permute-start.8
  84.8 7.2 %grad_q.1 = (bf16[512,1024]{1,0:T(8,128)(2,1)S(1)}, bf16[8,512,512]{2,1,0:T(8,128)(2,1)S(1)}, bf16[1,128,1024]{2,1,0:T(8,128)(2,1)S(1)}, bf16[1,128,1024]{2,1,0:T(8,128)(2,1)S(1)}) custom-call(s32[1,512]{1,0:T(1,128)S(1)} %bitcast.8, bf16[512,1024]{1,0:T(8,128)(2,1)S(1)} %get-tuple-element.61.g_ref, bf16[512,1024]{1,0:T(8,128)(2,1)S(1)} %get-tuple-element.52.k_ref, ...), custom_call_target="tpu_custom_call" | custom-call | flops 3000000000 | bytes 18432000 | tf_op jit(solution)/shard_map/grad_q/pallas_call | solution.py:469
  92.0 4.7 %inner.1 = (f32[512,1024]{1,0:T(8,128)S(1)}, f32[512,1024]{1,0:T(8,128)S(1)}) custom-call(bf16[8,512,512]{2,1,0:T(8,128)(2,1)S(1)} %get-tuple-element.67.z_ref, bf16[8,512,512]{2,1,0:T(8,128)(2,1)} %copy-done.19, bf16[512,1024]{1,0:T(8,128)(2,1)S(1)} %copy-done.4, bf16[512,1024]{1,0:T(8,128)(2,1)S(1)} %get-tuple-element.61.g_ref), custom_call_target="tpu_custom_call" | custom-call | flops 3000000000 | bytes 14336000 | tf_op jit(solution)/shard_map/inner/pallas_call | solution.py:513
  96.7 3.4 %grad_kv.1 = (bf16[512,1024]{1,0:T(8,128)(2,1)S(1)}, bf16[512,1024]{1,0:T(8,128)(2,1)S(1)}, bf16[2,128,1024]{2,1,0:T(8,128)(2,1)S(1)}, bf16[2,128,1024]{2,1,0:T(8,128)(2,1)S(1)}) custom-call(s32[1,512]{1,0:T(1,128)S(1)} %bitcast.9, bf16[8,144,128]{2,1,0:T(8,128)(2,1)S(1)} %collective-permute-done.8.near_ref, ...), custom_call_target="tpu_custom_call" | custom-call | flops 1000000000 | bytes 10240000 | tf_op jit(solution)/shard_map/grad_kv/pallas_call | solution.py:555
  100.1 7.3 %collective-permute-start.10 = (bf16[2,128,1024]{2,1,0:T(8,128)(2,1)S(1)}, bf16[2,128,1024]{2,1,0:T(8,128)(2,1)S(1)}, u32[]{:S(2)}, u32[]{:S(2)}) collective-permute-start(bf16[2,128,1024]{2,1,0:T(8,128)(2,1)S(1)} %get-tuple-element.74), channel_id=1, source_target_pairs={{0,4},{4,8},{8,12},{12,16},{16,20},{20,24},{24,28},{1,5},{5,9},{9,... | collective-permute-start | bytes 1572872 | tf_op jit(solution)/shard_map/ppermute | solution.py:649
  107.4 1.3 collective-permute-start.11
  108.7 4.6 %collective-permute-start.6 = (bf16[1,128,1024]{2,1,0:T(8,128)(2,1)S(1)}, bf16[1,128,1024]{2,1,0:T(8,128)(2,1)S(1)}, u32[]{:S(2)}, u32[]{:S(2)}) collective-permute-start(bf16[1,128,1024]{2,1,0:T(8,128)(2,1)S(1)} %get-tuple-element.63), channel_id=1, source_target_pairs={{0,4},{4,8},{8,12},{12,16},{16,20},{20,24},{24,28},{1,5},{5,9},{9,... | collective-permute-start | bytes 786440 | tf_op jit(solution)/shard_map/ppermute | solution.py:649
  113.3 1.3 collective-permute-start.7
  114.6 3.3 %own.1 = (bf16[512,1024]{1,0:T(8,128)(2,1)S(1)}, bf16[512,1024]{1,0:T(8,128)(2,1)S(1)}, bf16[512,1024]{1,0:T(8,128)(2,1)S(1)}) custom-call(s32[1,512]{1,0:T(1,128)S(1)} %bitcast.10, bf16[512,1024]{1,0:T(8,128)(2,1)S(1)} %get-tuple-element.65.refs_0_, bf16[512,1024]{1,0:T(8,128)(2,1)S(1)} %get-tuple-element.71.refs_1_, ...), custom_call_target="tpu_custom_call" | custom-call | flops 1620000000 | bytes 6291456 | tf_op jit(solution)/shard_map/own/pallas_call | solution.py:596
  117.8 22.6 %collective-permute-done.6.left_ref = bf16[1,128,1024]{2,1,0:T(8,128)(2,1)S(1)} collective-permute-done((bf16[1,128,1024]{2,1,0:T(8,128)(2,1)S(1)}, bf16[1,128,1024]{2,1,0:T(8,128)(2,1)S(1)}, u32[]{:S(2)}, u32[]{:S(2)}) %collective-permute-start.6) | collective-permute-done | bytes 262176 | tf_op jit(solution)/shard_map/ppermute | solution.py:649
  140.4 2.4 %finish.2 = bf16[512,1024]{1,0:T(8,128)(2,1)} custom-call(s32[2,128]{1,0:T(2,128)S(1)} %bitcast.5, bf16[1,128,1024]{2,1,0:T(8,128)(2,1)S(1)} %collective-permute-done.6.left_ref, bf16[1,128,1024]{2,1,0:T(8,128)(2,1)S(1)} %collective-permute-done.7.right_ref, bf16[512,1024]{1,0:T(8,128)(2,1)S(1)} %get-tuple-element.73.refs_0_), custom_call_target="tpu_custom_call" | custom-call | flops 270000000 | bytes 3072000 | tf_op jit(solution)/shard_map/finish/pallas_call | solution.py:634
  142.8 2.9 %finish.3 = (bf16[512,1024]{1,0:T(8,128)(2,1)}, bf16[512,1024]{1,0:T(8,128)(2,1)}) custom-call(s32[2,128]{1,0:T(2,128)S(1)} %bitcast.6, bf16[2,128,1024]{2,1,0:T(8,128)(2,1)S(1)} %collective-permute-done.10.left_ref, bf16[2,128,1024]{2,1,0:T(8,128)(2,1)S(1)} %collective-permute-done.11.right_ref, bf16[512,1024]{1,0:T(8,128)(2,1)S(1)} %get-tuple-element.76.refs_0_, ...), custom_call_target="tpu_custom_call" | custom-call | flops 540000000 | bytes 6144000 | tf_op jit(solution)/shard_map/finish/pallas_call | solution.py:634
  (51 shorter events, 9.3 us)
Async XLA Ops:
  0.6 23.6 %copy-start.20 = (s32[8]{0:T(128)S(1)}, s32[8]{0:T(128)}, u32[]{:S(2)}) copy-start(s32[8]{0:T(128)} %docs_ref.1) | copy-start | bytes 100
  0.6 1.2 copy-start.7
  2.6 21.7 %copy-start.8 = (bf16[512,1024]{1,0:T(8,128)(2,1)S(1)}, bf16[512,1024]{1,0:T(8,128)(2,1)}, u32[]{:S(2)}) copy-start(bf16[512,1024]{1,0:T(8,128)(2,1)} %refs_0_.2) | copy-start | bytes 3145732
  2.6 21.7 %copy-start.17 = (s32[512]{0:T(512)S(1)}, s32[512]{0:T(512)}, u32[]{:S(2)}) copy-start(s32[512]{0:T(512)} %param.15) | copy-start | bytes 6148
  4.8 50.8 %collective-permute-start = (bf16[1,128,1024]{2,1,0:T(8,128)(2,1)}, bf16[1,128,1024]{2,1,0:T(8,128)(2,1)S(1)}, u32[]{:S(2)}, u32[]{:S(2)}) collective-permute-start(bf16[1,128,1024]{2,1,0:T(8,128)(2,1)} %get-tuple-element.44), channel_id=1, source_target_pairs={{0,4},{4,8},{8,12},{12,16},{16,20},{20,24},{24,28},{1,5},{5,9},{9,... | collective-permute-start | bytes 786440 | tf_op jit(solution)/shard_map/ppermute | solution.py:649
  9.7 45.9 %collective-permute-start.1 = (bf16[1,128,1024]{2,1,0:T(8,128)(2,1)}, bf16[1,128,1024]{2,1,0:T(8,128)(2,1)}, u32[]{:S(2)}, u32[]{:S(2)}) collective-permute-start(bf16[1,128,1024]{2,1,0:T(8,128)(2,1)} %get-tuple-element.45), channel_id=1, source_target_pairs={{4,0},{8,4},{12,8},{16,12},{20,16},{24,20},{28,24},{5,1},{9,5},{13... | collective-permute-start | bytes 786440 | tf_op jit(solution)/shard_map/ppermute | solution.py:649
  11.0 1.2 copy-start.9
  12.2 1.2 copy-start.11
  14.1 9.3 %copy-start.21 = (f32[512,8]{0,1:T(8,128)S(1)}, f32[512,8]{0,1:T(8,128)}, u32[]{:S(2)}) copy-start(f32[512,8]{0,1:T(8,128)} %param.12) | copy-start | bytes 49156
  14.1 10.1 %copy-start.10 = (bf16[512,1024]{1,0:T(8,128)(2,1)S(1)}, bf16[512,1024]{1,0:T(8,128)(2,1)}, u32[]{:S(2)}) copy-start(bf16[512,1024]{1,0:T(8,128)(2,1)} %refs_0_.3) | copy-start | bytes 3145732
  16.7 26.9 %collective-permute-start.2 = (bf16[2,128,1024]{2,1,0:T(8,128)(2,1)}, bf16[2,128,1024]{2,1,0:T(8,128)(2,1)}, u32[]{:S(2)}, u32[]{:S(2)}) collective-permute-start(bf16[2,128,1024]{2,1,0:T(8,128)(2,1)} %get-tuple-element.48), channel_id=1, source_target_pairs={{0,4},{4,8},{8,12},{12,16},{16,20},{20,24},{24,28},{1,5},{5,9},{9,... | collective-permute-start | bytes 1572872 | tf_op jit(solution)/shard_map/ppermute | solution.py:649
  22.1 21.5 %collective-permute-start.3 = (bf16[2,128,1024]{2,1,0:T(8,128)(2,1)}, bf16[2,128,1024]{2,1,0:T(8,128)(2,1)}, u32[]{:S(2)}, u32[]{:S(2)}) collective-permute-start(bf16[2,128,1024]{2,1,0:T(8,128)(2,1)} %get-tuple-element.49), channel_id=1, source_target_pairs={{4,0},{8,4},{12,8},{16,12},{20,16},{24,20},{28,24},{5,1},{9,5},{13... | collective-permute-start | bytes 1572872 | tf_op jit(solution)/shard_map/ppermute | solution.py:649
  24.3 1.2 copy-start.12
  25.5 0.9 copy-start.13
  47.7 16.8 %collective-permute-start.5 = (bf16[8,144,128]{2,1,0:T(8,128)(2,1)S(1)}, bf16[8,144,128]{2,1,0:T(8,128)(2,1)S(1)}, u32[]{:S(2)}, u32[]{:S(2)}) collective-permute-start(bf16[8,144,128]{2,1,0:T(8,128)(2,1)S(1)} %get-tuple-element.57), channel_id=1, source_target_pairs={{0,8},{4,12},{8,16},{12,20},{16,24},{20,28},{1,9},{5,13},{9,17},{1... | collective-permute-start | bytes 884744 | tf_op jit(solution)/shard_map/ppermute | solution.py:649
  53.8 10.7 %collective-permute-start.4 = (bf16[8,144,128]{2,1,0:T(8,128)(2,1)S(1)}, bf16[8,144,128]{2,1,0:T(8,128)(2,1)S(1)}, u32[]{:S(2)}, u32[]{:S(2)}) collective-permute-start(bf16[8,144,128]{2,1,0:T(8,128)(2,1)S(1)} %get-tuple-element.57), channel_id=1, source_target_pairs={{0,4},{4,8},{8,12},{12,16},{16,20},{20,24},{24,28},{1,5},{5,9},{9,... | collective-permute-start | bytes 884744 | tf_op jit(solution)/shard_map/ppermute | solution.py:649
  55.6 8.8 %copy-start = (bf16[512,1024]{1,0:T(8,128)(2,1)S(1)}, bf16[512,1024]{1,0:T(8,128)(2,1)}, u32[]{:S(2)}) copy-start(bf16[512,1024]{1,0:T(8,128)(2,1)} %ct_ref.3) | copy-start | bytes 3145732
  55.6 8.8 %copy-start.18 = (f32[8]{0:T(128)S(1)}, f32[8]{0:T(128)}, u32[]{:S(2)}) copy-start(f32[8]{0:T(128)} %scale_ref.3) | copy-start | bytes 100
  62.4 2.0 %copy-start.19 = (bf16[8,512,512]{2,1,0:T(8,128)(2,1)}, bf16[8,512,512]{2,1,0:T(8,128)(2,1)S(1)}, u32[]{:S(2)}) copy-start(bf16[8,512,512]{2,1,0:T(8,128)(2,1)S(1)} %get-tuple-element.68.p_ref) | copy-start | bytes 12582916
  64.4 2.7 %copy-start.2 = (bf16[512,1024]{1,0:T(8,128)(2,1)}, bf16[512,1024]{1,0:T(8,128)(2,1)S(1)}, u32[]{:S(2)}) copy-start(bf16[512,1024]{1,0:T(8,128)(2,1)S(1)} %get-tuple-element.56.q_ref) | copy-start | bytes 3145732
  67.2 1.3 copy-start.5
  74.4 1.2 copy-start.1
  75.6 1.2 copy-start.3
  76.8 1.6 %copy-start.6 = (f32[512,1024]{1,0:T(8,128)S(1)}, f32[512,1024]{1,0:T(8,128)}, u32[]{:S(2)}) copy-start(f32[512,1024]{1,0:T(8,128)} %copy-done.5) | copy-start | bytes 6291460
  82.2 14.5 %collective-permute-start.9 = (bf16[8,144,128]{2,1,0:T(8,128)(2,1)S(1)}, bf16[8,144,128]{2,1,0:T(8,128)(2,1)S(1)}, u32[]{:S(2)}, u32[]{:S(2)}) collective-permute-start(bf16[8,144,128]{2,1,0:T(8,128)(2,1)S(1)} %get-tuple-element.66), channel_id=1, source_target_pairs={{8,0},{12,4},{16,8},{20,12},{24,16},{28,20},{9,1},{13,5},{17,9},{2... | collective-permute-start | bytes 884744 | tf_op jit(solution)/shard_map/ppermute | solution.py:649
  83.5 13.2 %collective-permute-start.8 = (bf16[8,144,128]{2,1,0:T(8,128)(2,1)S(1)}, bf16[8,144,128]{2,1,0:T(8,128)(2,1)S(1)}, u32[]{:S(2)}, u32[]{:S(2)}) collective-permute-start(bf16[8,144,128]{2,1,0:T(8,128)(2,1)S(1)} %get-tuple-element.66), channel_id=1, source_target_pairs={{4,0},{8,4},{12,8},{16,12},{20,16},{24,20},{28,24},{5,1},{9,5},{13... | collective-permute-start | bytes 884744 | tf_op jit(solution)/shard_map/ppermute | solution.py:649
  84.8 7.2 %copy-start.4 = (bf16[512,1024]{1,0:T(8,128)(2,1)S(1)}, bf16[512,1024]{1,0:T(8,128)(2,1)}, u32[]{:S(2)}) copy-start(bf16[512,1024]{1,0:T(8,128)(2,1)} %copy-done.2) | copy-start | bytes 3145732
  100.1 42.7 %collective-permute-start.10 = (bf16[2,128,1024]{2,1,0:T(8,128)(2,1)S(1)}, bf16[2,128,1024]{2,1,0:T(8,128)(2,1)S(1)}, u32[]{:S(2)}, u32[]{:S(2)}) collective-permute-start(bf16[2,128,1024]{2,1,0:T(8,128)(2,1)S(1)} %get-tuple-element.74), channel_id=1, source_target_pairs={{0,4},{4,8},{8,12},{12,16},{16,20},{20,24},{24,28},{1,5},{5,9},{9,... | collective-permute-start | bytes 1572872 | tf_op jit(solution)/shard_map/ppermute | solution.py:649
  107.4 35.4 %collective-permute-start.11 = (bf16[2,128,1024]{2,1,0:T(8,128)(2,1)S(1)}, bf16[2,128,1024]{2,1,0:T(8,128)(2,1)S(1)}, u32[]{:S(2)}, u32[]{:S(2)}) collective-permute-start(bf16[2,128,1024]{2,1,0:T(8,128)(2,1)S(1)} %get-tuple-element.75), channel_id=1, source_target_pairs={{4,0},{8,4},{12,8},{16,12},{20,16},{24,20},{28,24},{5,1},{9,5},{13... | collective-permute-start | bytes 1572872 | tf_op jit(solution)/shard_map/ppermute | solution.py:649
  108.7 31.7 %collective-permute-start.6 = (bf16[1,128,1024]{2,1,0:T(8,128)(2,1)S(1)}, bf16[1,128,1024]{2,1,0:T(8,128)(2,1)S(1)}, u32[]{:S(2)}, u32[]{:S(2)}) collective-permute-start(bf16[1,128,1024]{2,1,0:T(8,128)(2,1)S(1)} %get-tuple-element.63), channel_id=1, source_target_pairs={{0,4},{4,8},{8,12},{12,16},{16,20},{20,24},{24,28},{1,5},{5,9},{9,... | collective-permute-start | bytes 786440 | tf_op jit(solution)/shard_map/ppermute | solution.py:649
  113.3 27.1 %collective-permute-start.7 = (bf16[1,128,1024]{2,1,0:T(8,128)(2,1)S(1)}, bf16[1,128,1024]{2,1,0:T(8,128)(2,1)S(1)}, u32[]{:S(2)}, u32[]{:S(2)}) collective-permute-start(bf16[1,128,1024]{2,1,0:T(8,128)(2,1)S(1)} %get-tuple-element.64), channel_id=1, source_target_pairs={{4,0},{8,4},{12,8},{16,12},{20,16},{24,20},{28,24},{5,1},{9,5},{13... | collective-permute-start | bytes 786440 | tf_op jit(solution)/shard_map/ppermute | solution.py:649
  114.6 25.8 %copy-start.16 = (s32[1,2,128]{2,1,0:T(2,128)S(1)}, s32[1,2,128]{2,1,0:T(2,128)}, u32[]{:S(2)}) copy-start(s32[1,2,128]{2,1,0:T(2,128)} %param.14) | copy-start | bytes 3076
  (2 other events, 1.4 us)
where the time goes:
time: 148 us; the launch traced here: 146 us
  Pallas kernels  53.4 us (36%)
  starting transfers between devices  37.7 us (25%)
  waiting for transfers between devices  32.2 us (22%)
  local copies, waits for them, and re-layouts  15.4 us (10%)
  blocking collectives  5.93 us (4%)
    ppermute x12, starting transfers between devices, shifted(): lax.ppermute(array, 'seq', [(i, i + by) for i in range(peers) if 0 <= i +...  37.7 us
    ppermute x12, waiting for transfers between devices, shifted(): lax.ppermute(array, 'seq', [(i, i + by) for i in range(peers) if 0 <= i +...  32.2 us
    unnamed x45, local copies, waits for them, and re-layouts  15.4 us
    pallas_call x1, Pallas kernels, prep(): pl.pallas_call(prep_kernel, grid=(pairs,), in_specs=[smem, smem, whole2(1...  7.53 us
    pallas_call x1, Pallas kernels, grad_q(): pl.pallas_call(grad_q_kernel, grid=(pairs,), in_specs=[pl.BlockSpec((1, r...  7.17 us
    pallas_call x1, Pallas kernels, inside(): pl.pallas_call(inside_kernel, grid=(pairs,), in_specs=[pl.BlockSpec((rows...  6.76 us
    psum x1, blocking collectives, on_device(): sums = lax.psum(sums, 'head')  5.93 us
    pallas_call x2, Pallas kernels, finish(): pl.pallas_call(finish_kernel, grid=(features // cols,), in_specs=[pl.Bloc...  5.3 us
  transfers between devices with their start and end apart: 12, of which 2 were waited for; matrix products, arithmetic and copies ran while one was open for 1% of the time, Pallas kernels for 26%

commit v1 on v0

--- a/solution.py
+++ b/solution.py
@@ -11,7 +11,7 @@
 EPSILON = 1e-05
 LOG2E = math.log2(math.e)
 MASKED = -1e30
-VMEM_BYTES = 40 * 1024 * 1024
+MIB = 1024 * 1024
 BF = jnp.bfloat16
 F32 = jnp.float32
 NT = (((1,), (1,)), ((), ()))
@@ -42,37 +42,46 @@
     return jnp.where(hit, 1.0, 0.0).astype(BF)
 
 
-def params():
-    return pltpu.CompilerParams(vmem_limit_bytes=VMEM_BYTES)
-
-
-def cost(mflops, kbytes):
-    return pl.CostEstimate(
-        flops=int(mflops * 1e6), bytes_accessed=int(kbytes * 1024), transcendentals=0
-    )
+def in_hbm(shape, dtype):
+    return pltpu.HBM(shape, dtype)
+
+
+def stay(*arrays):
+    return [pltpu.with_memory_space_constraint(a, pltpu.HBM) for a in arrays]
+
+
+def params(mib=20):
+    return pltpu.CompilerParams(vmem_limit_bytes=mib * MIB)
+
+
+def planned(us):
+    return pl.CostEstimate(flops=int(us * 1.1e9), bytes_accessed=1_000_000, transcendentals=0)
+
+
+def pick_rows(hot_ref, sources, left_ref, right_ref):
+    capacity = left_ref.shape[1]
+    for index, source in enumerate(sources):
+        picked = dot(hot_ref[...], source[...]).astype(BF)
+        left_ref[index] = picked[:capacity]
+        right_ref[index] = picked[capacity:]
 
 
 def pick_kernel(send_ref, *refs):
-    count = len(refs) - 3
-    sources = refs[:count]
-    left_ref, right_ref, hot_ref = refs[count:]
+    *sources, left_ref, right_ref, hot_ref = refs
     rows = sources[0].shape[0]
     capacity = send_ref.shape[1]
 
     @pl.when(pl.program_id(0) == 0)
     def _():
-        lane = iota((capacity, rows), 1)
+        lane = iota((capacity, 128), 1)
         for side in range(2):
             named = along_rows(send_ref[side : side + 1, :], 128)
             for start in range(0, rows, 128):
                 hot_ref[side * capacity : (side + 1) * capacity, start : start + 128] = one_hot(
-                    named == lane[:, :128] + start
+                    named == lane + start
                 )
 
-    for index, source in enumerate(sources):
-        picked = dot(hot_ref[...], source[...]).astype(BF)
-        left_ref[index] = picked[:capacity]
-        right_ref[index] = picked[capacity:]
+    pick_rows(hot_ref, sources, left_ref, right_ref)
 
 
 def pick(send, arrays, cols):
@@ -86,27 +95,23 @@
         pick_kernel,
         grid=(features // cols,),
         in_specs=[pl.BlockSpec((2, capacity), lambda g: (0, 0))] + [block] * count,
-        out_specs=[out, out],
-        out_shape=[shape, shape],
-        scratch_shapes=[pltpu.VMEM((2 * capacity, rows), BF)],
-        compiler_params=params(),
-        cost_estimate=cost(268 * count, 1536 * count),
+        out_specs=[out, out, pl.BlockSpec((2 * capacity, rows), lambda g: (0, 0))],
+        out_shape=[shape, shape, in_hbm((2 * capacity, rows), BF)],
+        compiler_params=params(56),
+        cost_estimate=planned(2),
         name="pick",
     )(send, *arrays)
 
 
 def prep_kernel(
-    docs_ref, first_ref, take_ref, log_ref, q_ref, k_ref, v_ref,
-    qo_ref, ko_ref, vo_ref, hot_ref, weight_ref, cols_ref, through_ref,
-    own_ref, mask_ref, rows_ref,
+    docs_ref, first_ref, take_ref, log_ref, named_ref, q_ref, k_ref, v_ref,
+    left_ref, right_ref, qo_ref, ko_ref, vo_ref, hot_ref, mask_ref, cols_ref, rows_ref, through_ref, own_ref,
 ):
     rows = q_ref.shape[0]
     heads = log_ref.shape[1]
     capacity = hot_ref.shape[1] // 2
-    step = pl.program_id(0)
-    half = rows // 2
-
-    @pl.when(step == 0)
+
+    @pl.when(pl.program_id(0) == 0)
     def _():
         first = first_ref[0]
         position = first + iota((rows, 1), 0)
@@ -170,22 +175,14 @@
         hot_ref[:, :capacity] = one_hot(taken == lane)
         hot_ref[:, capacity:] = one_hot(taken - (capacity + rows) == lane)
 
+    pick_rows(named_ref, (q_ref,), left_ref, right_ref)
     own = own_ref[...]
     qo_ref[...] = dot(own, q_ref[...]).astype(BF)
     ko_ref[...] = dot(own, k_ref[...]).astype(BF)
     vo_ref[...] = dot(own, v_ref[...]).astype(BF)
-    for t in range(2):
-        column = cols_ref[step, :, 4 + t : 5 + t]
-        row = rows_ref[step, t : t + 1, :]
-        for i in range(2):
-            top, width = i * half, (i + 1) * half
-            weight_ref[t, top : top + half, :width] = jnp.exp2(
-                (column[top : top + half] - row[:, :width])
-                + mask_ref[top : top + half, :width]
-            )
-
-
-def prep(docs, first, take, log_decay, q, k, v, capacity):
+
+
+def prep(docs, first, take, log_decay, named, q, k, v, capacity):
     rows, features = q.shape
     heads = log_decay.shape[1]
     pairs = heads // 2
@@ -194,34 +191,37 @@
     block = pl.BlockSpec((rows, cols), lambda g: (0, g))
     whole2 = lambda a, b: pl.BlockSpec((a, b), lambda g: (0, 0))
     whole3 = lambda a, b, c: pl.BlockSpec((a, b, c), lambda g: (0, 0, 0))
+    side = pl.BlockSpec((1, capacity, cols), lambda g: (0, 0, g))
     own = jax.ShapeDtypeStruct((rows, features), BF)
+    slots = jax.ShapeDtypeStruct((1, capacity, features), BF)
     return pl.pallas_call(
         prep_kernel,
         grid=(pairs,),
-        in_specs=[smem, smem, whole2(1, rows), whole2(rows, heads), block, block, block],
+        in_specs=[
+            smem, smem, whole2(1, rows), whole2(rows, heads),
+            whole2(2 * capacity, rows), block, block, block,
+        ],
         out_specs=[
-            block, block, block,
+            side, side, block, block, block,
             whole2(rows, 2 * capacity),
-            pl.BlockSpec((2, rows, rows), lambda g: (g, 0, 0)),
+            whole2(rows, rows),
             whole3(pairs, rows, 8),
+            whole3(pairs, 8, rows),
             whole3(heads, 16, 128),
         ],
         out_shape=[
-            own, own, own,
+            slots, slots, own, own, own,
             jax.ShapeDtypeStruct((rows, 2 * capacity), BF),
-            jax.ShapeDtypeStruct((heads, rows, rows), F32),
-            jax.ShapeDtypeStruct((pairs, rows, 8), F32),
-            jax.ShapeDtypeStruct((heads, 16, 128), BF),
-        ],
-        scratch_shapes=[
-            pltpu.VMEM((rows, rows), BF),
-            pltpu.VMEM((rows, rows), F32),
-            pltpu.VMEM((pairs, 8, rows), F32),
-        ],
-        compiler_params=params(),
-        cost_estimate=cost(6000, 16000),
+            in_hbm((rows, rows), F32),
+            in_hbm((pairs, rows, 8), F32),
+            in_hbm((pairs, 8, rows), F32),
+            in_hbm((heads, 16, 128), BF),
+        ],
+        scratch_shapes=[pltpu.VMEM((rows, rows), BF)],
+        compiler_params=params(),
+        cost_estimate=planned(30),
         name="prep",
-    )(docs, first, take, log_decay, q, k, v)
+    )(docs, first, take, log_decay, *stay(named, q, k, v))
 
 
 def arrived(own_ref, hot_ref, left, right):
@@ -251,7 +251,7 @@
     capacity = left.shape[1]
     block = pl.BlockSpec((rows, width), lambda g: (0, g))
     side = pl.BlockSpec((2, capacity, width), lambda g: (0, 0, g))
-    full = jax.ShapeDtypeStruct((rows, features), BF)
+    full = in_hbm((rows, features), BF)
     return pl.pallas_call(
         state_kernel,
         grid=(pairs,),
@@ -264,12 +264,18 @@
         out_specs=[block, block, pl.BlockSpec((2, dk + 16, dk), lambda g: (g, 0, 0))],
         out_shape=[full, full, jax.ShapeDtypeStruct((heads, dk + 16, dk), BF)],
         compiler_params=params(),
-        cost_estimate=cost(2000, 6000),
+        cost_estimate=planned(30),
         name="state",
-    )(hot, k_own, v_own, left, right, cols, through)
-
-
-def inside_kernel(hot_ref, qo_ref, left_ref, right_ref, k_ref, v_ref, weight_ref, q_ref, p_ref, o_ref):
+    )(hot, k_own, v_own, left, right, *stay(cols, through))
+
+
+def decay(cols_ref, rows_ref, mask_ref, t, top, half, reach):
+    column = cols_ref[0, top : top + half, 4 + t : 5 + t]
+    row = rows_ref[0, t : t + 1, :reach]
+    return jnp.exp2((column - row) + mask_ref[top : top + half, :reach])
+
+
+def inside_kernel(hot_ref, qo_ref, left_ref, right_ref, k_ref, v_ref, mask_ref, cols_ref, rows_ref, q_ref, o_ref):
     rows, width = k_ref.shape
     dk, half = width // 2, rows // 2
     q = arrived(qo_ref, hot_ref, left_ref[0], right_ref[0])
@@ -279,37 +285,42 @@
         for i in range(2):
             top, reach = i * half, (i + 1) * half
             scores = dot_nt(q[top : top + half, part], k_ref[:reach, part])
-            p = (scores * weight_ref[t, top : top + half, :reach]).astype(BF)
-            p_ref[t, top : top + half, :reach] = p
+            weight = decay(cols_ref, rows_ref, mask_ref, t, top, half, reach)
+            p = (scores * weight).astype(BF)
             o_ref[top : top + half, part] = dot(p, v_ref[:reach, part])
 
 
-def inside(hot, q_own, left, right, k, v, weight):
+def tables(rows):
+    return [
+        pl.BlockSpec((rows, rows), lambda g: (0, 0)),
+        pl.BlockSpec((1, rows, 8), lambda g: (g, 0, 0)),
+        pl.BlockSpec((1, 8, rows), lambda g: (g, 0, 0)),
+    ]
+
+
+def inside(hot, q_own, left, right, k, v, mask, cols, turned):
     rows, features = k.shape
-    heads = weight.shape[0]
-    pairs = heads // 2
+    pairs = cols.shape[0]
     width = features // pairs
     capacity = left.shape[1]
     block = pl.BlockSpec((rows, width), lambda g: (0, g))
     side = pl.BlockSpec((1, capacity, width), lambda g: (0, 0, g))
-    square = pl.BlockSpec((2, rows, rows), lambda g: (g, 0, 0))
     return pl.pallas_call(
         inside_kernel,
         grid=(pairs,),
         in_specs=[
             pl.BlockSpec((rows, 2 * capacity), lambda g: (0, 0)),
-            block, side, side, block, block, square,
-        ],
-        out_specs=[block, square, block],
+            block, side, side, block, block, *tables(rows),
+        ],
+        out_specs=[block, block],
         out_shape=[
-            jax.ShapeDtypeStruct((rows, features), BF),
-            jax.ShapeDtypeStruct((heads, rows, rows), BF),
+            in_hbm((rows, features), BF),
             jax.ShapeDtypeStruct((rows, features), F32),
         ],
         compiler_params=params(),
-        cost_estimate=cost(3000, 18000),
+        cost_estimate=planned(30),
         name="inside",
-    )(hot, q_own, left, right, k, v, weight)
+    )(hot, q_own, left, right, *stay(k, v, mask, cols, turned))
 
 
 def joined(near_ref, far_ref, t, dk):
@@ -368,15 +379,15 @@
             pl.BlockSpec((2, rows), lambda g: (0, 0)),
         ],
         out_shape=[
-            jax.ShapeDtypeStruct((rows, features), F32),
-            jax.ShapeDtypeStruct((2 * pairs, dk, dk), BF),
+            in_hbm((rows, features), F32),
+            in_hbm((2 * pairs, dk, dk), BF),
             jax.ShapeDtypeStruct((2, rows), F32),
         ],
         scratch_shapes=[pltpu.VMEM((rows, dk), F32), pltpu.VMEM((rows, dk), F32)],
         compiler_params=params(),
-        cost_estimate=cost(400, 8000),
+        cost_estimate=planned(3),
         name="output",
-    )(head_scale, o, q, near, far, cols, ct)
+    )(head_scale, o, *stay(q), near, far, *stay(cols, ct))
 
 
 def norm_kernel(total, scale_ref, sums_ref, u_ref, ct_ref, q_ref, cols_ref, through_ref, n_ref, g_ref, s_ref, inv_ref, mean_ref):
@@ -422,9 +433,9 @@
         out_shape=[full, full, jax.ShapeDtypeStruct((2 * pairs, dk + 16, dk), BF)],
         scratch_shapes=[pltpu.VMEM((rows, dk), F32), pltpu.VMEM((rows, dk), F32)],
         compiler_params=params(),
-        cost_estimate=cost(400, 8000),
+        cost_estimate=planned(4),
         name="norm",
-    )(head_scale, sums, u, ct, q, cols, through)
+    )(head_scale, sums, *stay(u, ct, q, cols, through))
 
 
 def slots_hot(take_ref, hot_ref, capacity, rows):
@@ -434,7 +445,7 @@
     hot_ref[capacity:, :] = one_hot(taken - (capacity + rows) == slot)
 
 
-def grad_q_kernel(take_ref, g_ref, k_ref, v_ref, h_ref, weight_ref, cols_ref, dq_ref, z_ref, left_ref, right_ref, hot_ref):
+def grad_inner_kernel(take_ref, g_ref, q_ref, k_ref, v_ref, h_ref, mask_ref, cols_ref, rows_ref, dq_ref, dk_ref, dv_ref, left_ref, right_ref, hot_ref):
     rows, width = k_ref.shape
     dk, half = width // 2, rows // 2
     capacity = left_ref.shape[1]
@@ -445,81 +456,56 @@
 
     for t in range(2):
         part = slice(t * dk, (t + 1) * dk)
-        for i in range(2):
+        for i in (1, 0):
             top, reach = i * half, (i + 1) * half
-            g = g_ref[top : top + half, part]
-            scores = dot_nt(g, v_ref[:reach, part])
-            z = (scores * weight_ref[t, top : top + half, :reach]).astype(BF)
-            z_ref[t, top : top + half, :reach] = z
-            outer = dot_nt(g, h_ref[t]) * cols_ref[0, top : top + half, 2 + t : 3 + t]
-            dq_ref[top : top + half, part] = (dot(z, k_ref[:reach, part]) + outer).astype(BF)
+            here = slice(top, top + half)
+            g, q = g_ref[here, part], q_ref[here, part]
+            k, v = k_ref[:reach, part], v_ref[:reach, part]
+            weight = decay(cols_ref, rows_ref, mask_ref, t, top, half, reach)
+            z = (dot_nt(g, v) * weight).astype(BF)
+            p = (dot_nt(q, k) * weight).astype(BF)
+            outer = dot_nt(g, h_ref[t]) * cols_ref[0, here, 2 + t : 3 + t]
+            dq_ref[here, part] = (dot(z, k) + outer).astype(BF)
+            if i:
+                dk_ref[:reach, part] = dot_tn(z, q)
+                dv_ref[:reach, part] = dot_tn(p, g)
+            else:
+                dk_ref[:reach, part] += dot_tn(z, q)
+                dv_ref[:reach, part] += dot_tn(p, g)
     back = dot(hot_ref[...], dq_ref[...]).astype(BF)
     left_ref[0] = back[:capacity]
     right_ref[0] = back[capacity:]
 
 
-def grad_q(take, g, k, v, h, weight, cols, capacity):
+def grad_inner(take, g, q, k, v, h, mask, cols, turned, capacity):
     rows, features = k.shape
     pairs = cols.shape[0]
     width = features // pairs
     dk = width // 2
     block = pl.BlockSpec((rows, width), lambda g: (0, g))
     side = pl.BlockSpec((1, capacity, width), lambda g: (0, 0, g))
-    square = pl.BlockSpec((2, rows, rows), lambda g: (g, 0, 0))
-    return pl.pallas_call(
-        grad_q_kernel,
+    full = jax.ShapeDtypeStruct((rows, features), F32)
+    return pl.pallas_call(
+        grad_inner_kernel,
         grid=(pairs,),
         in_specs=[
             pl.BlockSpec((1, rows), lambda g: (0, 0)),
-            block, block, block,
+            block, block, block, block,
             pl.BlockSpec((2, dk, dk), lambda g: (g, 0, 0)),
-            square,
-            pl.BlockSpec((1, rows, 8), lambda g: (g, 0, 0)),
-        ],
-        out_specs=[block, square, side, side],
+            *tables(rows),
+        ],
+        out_specs=[block, block, block, side, side],
         out_shape=[
             jax.ShapeDtypeStruct((rows, features), BF),
-            jax.ShapeDtypeStruct((2 * pairs, rows, rows), BF),
+            full, full,
             jax.ShapeDtypeStruct((1, capacity, features), BF),
             jax.ShapeDtypeStruct((1, capacity, features), BF),
         ],
         scratch_shapes=[pltpu.VMEM((2 * capacity, rows), BF)],
         compiler_params=params(),
-        cost_estimate=cost(3000, 18000),
-        name="grad_q",
-    )(take, g, k, v, h, weight, cols)
-
-
-def inner_kernel(z_ref, p_ref, q_ref, g_ref, dk_ref, dv_ref):
-    rows, width = q_ref.shape
-    dk, half = width // 2, rows // 2
-    for t in range(2):
-        part = slice(t * dk, (t + 1) * dk)
-        for square, source, target in ((z_ref, q_ref, dk_ref), (p_ref, g_ref, dv_ref)):
-            for j in range(2):
-                top = j * half
-                target[top : top + half, part] = dot_tn(
-                    square[t, top:, top : top + half], source[top:, part]
-                )
-
-
-def inner(z, p, q, g):
-    rows, features = q.shape
-    heads = z.shape[0]
-    pairs = heads // 2
-    block = pl.BlockSpec((rows, features // pairs), lambda g: (0, g))
-    square = pl.BlockSpec((2, rows, rows), lambda g: (g, 0, 0))
-    full = jax.ShapeDtypeStruct((rows, features), F32)
-    return pl.pallas_call(
-        inner_kernel,
-        grid=(pairs,),
-        in_specs=[square, square, block, block],
-        out_specs=[block, block],
-        out_shape=[full, full],
-        compiler_params=params(),
-        cost_estimate=cost(3000, 14000),
-        name="inner",
-    )(z, p, q, g)
+        cost_estimate=planned(30),
+        name="grad_inner",
+    )(take, g, *stay(q, k, v, h, mask, cols, turned))
 
 
 def grad_kv_kernel(take_ref, near_ref, far_ref, k_ref, v_ref, cols_ref, dki_ref, dvi_ref, dk_ref, dv_ref, left_ref, right_ref, hot_ref):
@@ -569,13 +555,12 @@
         ],
         scratch_shapes=[pltpu.VMEM((2 * capacity, rows), BF)],
         compiler_params=params(),
-        cost_estimate=cost(1000, 10000),
+        cost_estimate=planned(30),
         name="grad_kv",
-    )(take, near, far, k, v, cols, dk_inner, dv_inner)
-
-
-def own_kernel(capacity, take_ref, *refs):
-    count = (len(refs) - 1) // 2
+    )(take, near, far, *stay(k, v, cols), dk_inner, dv_inner)
+
+
+def own_kernel(capacity, count, take_ref, *refs):
     hot_ref = refs[-1]
     rows = refs[0].shape[0]
 
@@ -584,26 +569,29 @@
         taken = jnp.broadcast_to(take_ref[...], (rows, rows))
         hot_ref[...] = one_hot(taken - capacity == iota((rows, rows), 0))
 
-    for source, target in zip(refs[:count], refs[count : 2 * count]):
+    for source, target in zip(refs[:count], refs[-1 - count : -1]):
         target[...] = dot(hot_ref[...], source[...]).astype(BF)
 
 
-def own(take, arrays, capacity, cols):
+def own(take, arrays, capacity, cols, after=None):
     rows, features = arrays[0].shape
     count = len(arrays)
     block = pl.BlockSpec((rows, cols), lambda g: (0, g))
     full = jax.ShapeDtypeStruct((rows, features), BF)
-    return pl.pallas_call(
-        functools.partial(own_kernel, capacity),
+    later = [] if after is None else [after]
+    return pl.pallas_call(
+        functools.partial(own_kernel, capacity, count),
         grid=(features // cols,),
-        in_specs=[pl.BlockSpec((1, rows), lambda g: (0, 0))] + [block] * count,
+        in_specs=[pl.BlockSpec((1, rows), lambda g: (0, 0))]
+        + [block] * count
+        + [pl.BlockSpec((16, 128), lambda g: (0, 0))] * len(later),
         out_specs=[block] * count,
         out_shape=[full] * count,
         scratch_shapes=[pltpu.VMEM((rows, rows), BF)],
         compiler_params=params(),
-        cost_estimate=cost(540 * count, 2048 * count),
+        cost_estimate=planned(2),
         name="own",
-    )(take, *arrays)
+    )(take, *arrays, *later)
 
 
 def finish_kernel(send_ref, left_ref, right_ref, *refs):
@@ -639,7 +627,7 @@
         out_shape=[full] * count,
         scratch_shapes=[pltpu.VMEM((rows, 2 * capacity), BF)],
         compiler_params=params(),
-        cost_estimate=cost(270 * count, 3000 * count),
+        cost_estimate=planned(2),
         name="finish",
     )(send, left, right, *arrays)
 
@@ -680,29 +668,30 @@
     first = (lax.axis_index("seq") * rows).astype(jnp.int32).reshape(1)
     total = features * lax.axis_size("head")
 
-    kv_left, kv_right = pick(send, (key_vectors, value_vectors), cols)
-    q_left, q_right = pick(send, (queries,), cols)
+    kv_left, kv_right, named = pick(send, (key_vectors, value_vectors), cols)
     kv_before, kv_after = shifted(kv_right, 1), shifted(kv_left, -1)
+    q_left, q_right, q_own, k_own, v_own, hot, mask, columns, turned, through = prep(
+        doc_lengths, first, take, log_decay, named, queries, key_vectors, value_vectors, capacity
+    )
     q_before, q_after = shifted(q_right, 1), shifted(q_left, -1)
-    q_own, k_own, v_own, hot, weight, columns, through = prep(
-        doc_lengths, first, take, log_decay, queries, key_vectors, value_vectors, capacity
-    )
     k, v, message = state(hot, k_own, v_own, kv_before, kv_after, columns, through)
     near, far = carried(message, 1)
-    q, probs, o_inside = inside(hot, q_own, q_before, q_after, k, v, weight)
+    q, o_inside = inside(hot, q_own, q_before, q_after, k, v, mask, columns, turned)
     u, state_low, sums = output(head_scale, o_inside, q, near, far, columns, cotangent)
     sums = lax.psum(sums, "head")
     normed, g, grad_message = norm(total, head_scale, sums, u, cotangent, q, columns, through)
     grad_near, grad_far = carried(grad_message, -1)
-    dq, z, dq_left, dq_right = grad_q(take, g, k, v, state_low, weight, columns, capacity)
+    dq, dk_inner, dv_inner, dq_left, dq_right = grad_inner(
+        take, g, q, k, v, state_low, mask, columns, turned, capacity
+    )
     dq_before, dq_after = shifted(dq_right, 1), shifted(dq_left, -1)
-    dk_inner, dv_inner = inner(z, probs, q, g)
     dk, dv, kv_left, kv_right = grad_kv(
         take, grad_near, grad_far, k, v, columns, dk_inner, dv_inner, capacity
     )
     dkv_before, dkv_after = shifted(kv_right, 1), shifted(kv_left, -1)
-    dq_own, dk_own, dv_own = own(take, (dq, dk, dv), capacity, cols)
+    (dq_own,) = own(take, (dq,), capacity, cols, dk)
     (grad_queries,) = finish(send, dq_before, dq_after, (dq_own,), cols)
+    dk_own, dv_own = own(take, (dk, dv), capacity, cols, *stay(grad_queries))
     grad_keys, grad_values = finish(send, dkv_before, dkv_after, (dk_own, dv_own), cols)
     return normed, grad_queries, grad_keys, grad_values
 

time: 148 us -> 133 us (0.90)
  the two profiles are of different devices: /device:TPU:0 before, /device:TPU:25 now
where the time goes in v1:
time: 133 us; the launch traced here: 132 us
  Pallas kernels  56.8 us (43%)
  starting transfers between devices  37.3 us (28%)
  waiting for transfers between devices  30.4 us (23%)
  blocking collectives  6.6 us (5%)
    ppermute x12, starting transfers between devices, shifted(): lax.ppermute(array, 'seq', [(i, i + by) for i in range(peers) if 0 <= i +...  37.3 us
    ppermute x12, waiting for transfers between devices, shifted(): lax.ppermute(array, 'seq', [(i, i + by) for i in range(peers) if 0 <= i +...  30.4 us
    pallas_call x1, Pallas kernels, grad_inner(): pl.pallas_call(grad_inner_kernel, grid=(pairs,), in_specs=[pl.BlockSpec((...  9.36 us
    pallas_call x1, Pallas kernels, prep(): pl.pallas_call(prep_kernel, grid=(pairs,), in_specs=[smem, smem, whole2(1...  8.19 us
    psum x1, blocking collectives, on_device(): sums = lax.psum(sums, 'head')  6.6 us
    pallas_call x1, Pallas kernels, inside(): pl.pallas_call(inside_kernel, grid=(pairs,), in_specs=[pl.BlockSpec((rows...  6.16 us
    pallas_call x2, Pallas kernels, finish(): pl.pallas_call(finish_kernel, grid=(features // cols,), in_specs=[pl.Bloc...  5.28 us
    pallas_call x1, Pallas kernels, norm(): pl.pallas_call(functools.partial(norm_kernel, total), grid=(pairs,), in_s...  5.03 us
  transfers between devices with their start and end apart: 12, of which 5 were waited for; matrix products, arithmetic and copies ran while one was open for 0% of the time, Pallas kernels for 30%

profile of v1, /device:TPU:25, one launch (start us, length us, event | category | flops | bytes accessed | tf_op | source)
XLA Modules:
  0.0 132.2 jit_solution(16298029090650432651)
XLA Ops:
  0.7 4.2 %pick.1 = (bf16[2,128,1024]{2,1,0:T(8,128)(2,1)}, bf16[2,128,1024]{2,1,0:T(8,128)(2,1)}, bf16[256,512]{1,0:T(8,128)(2,1)}) custom-call(s32[2,128]{1,0:T(2,128)} %bitcast.8, bf16[512,1024]{1,0:T(8,128)(2,1)} %k_ref.1, bf16[512,1024]{1,0:T(8,128)(2,1)} %v_ref.1), custom_call_target="tpu_custom_call" | custom-call | flops 2200000000 | bytes 1000000 | tf_op jit(solution)/shard_map/pick/pallas_call | solution.py:94
  4.8 3.1 %collective-permute-start.2 = (bf16[2,128,1024]{2,1,0:T(8,128)(2,1)}, bf16[2,128,1024]{2,1,0:T(8,128)(2,1)S(1)}, u32[]{:S(2)}, u32[]{:S(2)}) collective-permute-start(bf16[2,128,1024]{2,1,0:T(8,128)(2,1)} %get-tuple-element.48), channel_id=1, source_target_pairs={{0,4},{4,8},{8,12},{12,16},{16,20},{20,24},{24,28},{1,5},{5,9},{9,... | collective-permute-start | bytes 1572872 | tf_op jit(solution)/shard_map/ppermute | solution.py:637
  8.0 3.0 %collective-permute-start.3 = (bf16[2,128,1024]{2,1,0:T(8,128)(2,1)}, bf16[2,128,1024]{2,1,0:T(8,128)(2,1)S(1)}, u32[]{:S(2)}, u32[]{:S(2)}) collective-permute-start(bf16[2,128,1024]{2,1,0:T(8,128)(2,1)} %get-tuple-element.49), channel_id=1, source_target_pairs={{4,0},{8,4},{12,8},{16,12},{20,16},{24,20},{28,24},{5,1},{9,5},{13... | collective-permute-start | bytes 1572872 | tf_op jit(solution)/shard_map/ppermute | solution.py:637
  11.0 0.1 copy.13.log_ref
  11.2 8.2 %prep.1 = (bf16[1,128,1024]{2,1,0:T(8,128)(2,1)S(1)}, bf16[1,128,1024]{2,1,0:T(8,128)(2,1)S(1)}, bf16[512,1024]{1,0:T(8,128)(2,1)S(1)}, bf16[512,1024]{1,0:T(8,1...) custom-call(s32[8]{0:T(128)S(1)} %copy-done.2, ...), custom_call_target="tpu_custom_call" | custom-call | flops 32999999488 | bytes 1000000 | tf_op jit(solution)/shard_map/prep/pallas_call | solution.py:197
  19.4 2.3 %collective-permute-start = (bf16[1,128,1024]{2,1,0:T(8,128)(2,1)S(1)}, bf16[1,128,1024]{2,1,0:T(8,128)(2,1)S(1)}, u32[]{:S(2)}, u32[]{:S(2)}) collective-permute-start(bf16[1,128,1024]{2,1,0:T(8,128)(2,1)S(1)} %get-tuple-element.44), channel_id=1, source_target_pairs={{0,4},{4,8},{8,12},{12,16},{16,20},{20,24},{24,28},{1,5},{5,9},{9,... | collective-permute-start | bytes 786440 | tf_op jit(solution)/shard_map/ppermute | solution.py:637
  21.7 3.9 %collective-permute-start.1 = (bf16[1,128,1024]{2,1,0:T(8,128)(2,1)S(1)}, bf16[1,128,1024]{2,1,0:T(8,128)(2,1)S(1)}, u32[]{:S(2)}, u32[]{:S(2)}) collective-permute-start(bf16[1,128,1024]{2,1,0:T(8,128)(2,1)S(1)} %get-tuple-element.45), channel_id=1, source_target_pairs={{4,0},{8,4},{12,8},{16,12},{20,16},{24,20},{28,24},{5,1},{9,5},{13... | collective-permute-start | bytes 786440 | tf_op jit(solution)/shard_map/ppermute | solution.py:637
  25.6 13.0 %collective-permute-done.3.right_ref = bf16[2,128,1024]{2,1,0:T(8,128)(2,1)S(1)} collective-permute-done((bf16[2,128,1024]{2,1,0:T(8,128)(2,1)}, bf16[2,128,1024]{2,1,0:T(8,128)(2,1)S(1)}, u32[]{:S(2)}, u32[]{:S(2)}) %collective-permute-start.3) | collective-permute-done | bytes 524320 | tf_op jit(solution)/shard_map/ppermute | solution.py:637
  38.5 4.6 %state.1 = (bf16[512,1024]{1,0:T(8,128)(2,1)}, bf16[512,1024]{1,0:T(8,128)(2,1)}, bf16[8,144,128]{2,1,0:T(8,128)(2,1)S(1)}) custom-call(bf16[512,256]{1,0:T(8,128)(2,1)S(1)} %get-tuple-element.42.hot_ref, bf16[512,1024]{1,0:T(8,128)(2,1)S(1)} %get-tuple-element.46.ko_ref, bf16[512,1024]{1,0:T(8,128)(2,1)S(1)} %get-tuple-element.47.vo_ref, ...), custom_call_target="tpu_custom_call" | custom-call | flops 32999999488 | bytes 1000000 | tf_op jit(solution)/shard_map/state/pallas_call | solution.py:255
  43.1 1.9 %collective-permute-start.4 = (bf16[8,144,128]{2,1,0:T(8,128)(2,1)S(1)}, bf16[8,144,128]{2,1,0:T(8,128)(2,1)S(1)}, u32[]{:S(2)}, u32[]{:S(2)}) collective-permute-start(bf16[8,144,128]{2,1,0:T(8,128)(2,1)S(1)} %get-tuple-element.58), channel_id=1, source_target_pairs={{0,4},{4,8},{8,12},{12,16},{16,20},{20,24},{24,28},{1,5},{5,9},{9,... | collective-permute-start | bytes 884744 | tf_op jit(solution)/shard_map/ppermute | solution.py:637
  45.0 1.3 collective-permute-start.5
  46.3 0.0 copy-start.3
  46.4 6.2 %inside.1 = (bf16[512,1024]{1,0:T(8,128)(2,1)}, f32[512,1024]{1,0:T(8,128)S(1)}) custom-call(bf16[512,256]{1,0:T(8,128)(2,1)S(1)} %get-tuple-element.42.hot_ref, bf16[512,1024]{1,0:T(8,128)(2,1)S(1)} %get-tuple-element.43.qo_ref, bf16[1,128,1024]{2,1,0:T(8,128)(2,1)S(1)} %collective-permute-done.left_ref, ...), custom_call_target="tpu_custom_call" | custom-call | flops 32999999488 | bytes 1000000 | tf_op jit(solution)/shard_map/inside/pallas_call | solution.py:308
  52.5 1.3 %collective-permute-done.4.near_ref = bf16[8,144,128]{2,1,0:T(8,128)(2,1)S(1)} collective-permute-done((bf16[8,144,128]{2,1,0:T(8,128)(2,1)S(1)}, bf16[8,144,128]{2,1,0:T(8,128)(2,1)S(1)}, u32[]{:S(2)}, u32[]{:S(2)}) %collective-permute-start.4) | collective-permute-done | bytes 294944 | tf_op jit(solution)/shard_map/ppermute | solution.py:637
  53.8 0.9 collective-permute-done.5.far_ref
  54.8 5.0 %output.1 = (f32[512,1024]{1,0:T(8,128)}, bf16[8,128,128]{2,1,0:T(8,128)(2,1)}, f32[2,512]{1,0:T(2,128)S(1)}) custom-call(f32[8]{0:T(128)S(1)} %copy-done.3, f32[512,1024]{1,0:T(8,128)S(1)} %get-tuple-element.56.o_ref, bf16[512,1024]{1,0:T(8,128)(2,1)} %get-tuple-element.57.q_ref, bf16[8,144,128]{2,1,0:T(8,128)(2,1)S(1)} %collective-permute-done.4.near_ref, ...), custom_call_target="tpu_custom_call" | custom-call | flops 3300000000 | bytes 1000000 | tf_op jit(solution)/shard_map/output/pallas_call | solution.py:367
  59.8 6.6 %psum.7.sums_ref = f32[2,512]{1,0:T(2,128)S(1)} all-reduce(f32[2,512]{1,0:T(2,128)S(1)} %get-tuple-element.59), channel_id=1, replica_groups=mesh['seq'=8,'head'=4] {'head'}, use_global_device_ids=true, to_apply=%region_0.0 | all-reduce | flops 1024 | bytes 8192 | tf_op jit(solution)/shard_map/psum | solution.py:681
  66.4 5.0 %norm.1 = (bf16[512,1024]{1,0:T(8,128)(2,1)}, bf16[512,1024]{1,0:T(8,128)(2,1)S(1)}, bf16[8,144,128]{2,1,0:T(8,128)(2,1)S(1)}) custom-call(f32[8]{0:T(128)S(1)} %copy-done.3, f32[2,512]{1,0:T(2,128)S(1)} %psum.7.sums_ref, f32[512,1024]{1,0:T(8,128)} %get-tuple-element.60.u_ref, bf16[512,1024]{1,0:T(8,128)(2,1)} %ct_ref.3, ...), custom_call_target="tpu_custom_call" | custom-call | flops 4400000000 | bytes 1000000 | tf_op jit(solution)/shard_map/norm/pallas_call | solution.py:422
  71.4 7.3 %collective-permute-start.8 = (bf16[8,144,128]{2,1,0:T(8,128)(2,1)S(1)}, bf16[8,144,128]{2,1,0:T(8,128)(2,1)S(1)}, u32[]{:S(2)}, u32[]{:S(2)}) collective-permute-start(bf16[8,144,128]{2,1,0:T(8,128)(2,1)S(1)} %get-tuple-element.67), channel_id=1, source_target_pairs={{4,0},{8,4},{12,8},{16,12},{20,16},{24,20},{28,24},{5,1},{9,5},{13... | collective-permute-start | bytes 884744 | tf_op jit(solution)/shard_map/ppermute | solution.py:637
  78.7 2.1 %collective-permute-start.9 = (bf16[8,144,128]{2,1,0:T(8,128)(2,1)S(1)}, bf16[8,144,128]{2,1,0:T(8,128)(2,1)S(1)}, u32[]{:S(2)}, u32[]{:S(2)}) collective-permute-start(bf16[8,144,128]{2,1,0:T(8,128)(2,1)S(1)} %get-tuple-element.67), channel_id=1, source_target_pairs={{8,0},{12,4},{16,8},{20,12},{24,16},{28,20},{9,1},{13,5},{17,9},{2... | collective-permute-start | bytes 884744 | tf_op jit(solution)/shard_map/ppermute | solution.py:637
  80.8 9.4 %grad_inner.1 = (bf16[512,1024]{1,0:T(8,128)(2,1)S(1)}, f32[512,1024]{1,0:T(8,128)S(1)}, f32[512,1024]{1,0:T(8,128)S(1)}, bf16[1,128,1024]{2,1,0:T(8,128)(2,1)S(1)}, bf16[1,128,1024]{2,1,0:T(8,128)(2,1)S(1)}) custom-call(s32[1,512]{1,0:T(1,128)S(1)} %bitcast.4, bf16[512,1024]{1,0:T(8,128)(2,1)S(1)} %get-tuple-element.62.g_ref, ...), custom_call_target="tpu_custom_call" | custom-call | flops 32999999488 | bytes 1000000 | tf_op jit(solution)/shard_map/grad_inner/pallas_call | solution.py:488
  90.2 2.0 %collective-permute-start.6 = (bf16[1,128,1024]{2,1,0:T(8,128)(2,1)S(1)}, bf16[1,128,1024]{2,1,0:T(8,128)(2,1)S(1)}, u32[]{:S(2)}, u32[]{:S(2)}) collective-permute-start(bf16[1,128,1024]{2,1,0:T(8,128)(2,1)S(1)} %get-tuple-element.64), channel_id=1, source_target_pairs={{0,4},{4,8},{8,12},{12,16},{16,20},{20,24},{24,28},{1,5},{5,9},{9,... | collective-permute-start | bytes 786440 | tf_op jit(solution)/shard_map/ppermute | solution.py:637
  92.2 4.2 %collective-permute-start.7 = (bf16[1,128,1024]{2,1,0:T(8,128)(2,1)S(1)}, bf16[1,128,1024]{2,1,0:T(8,128)(2,1)S(1)}, u32[]{:S(2)}, u32[]{:S(2)}) collective-permute-start(bf16[1,128,1024]{2,1,0:T(8,128)(2,1)S(1)} %get-tuple-element.65), channel_id=1, source_target_pairs={{4,0},{8,4},{12,8},{16,12},{20,16},{24,20},{28,24},{5,1},{9,5},{13... | collective-permute-start | bytes 786440 | tf_op jit(solution)/shard_map/ppermute | solution.py:637
  96.4 4.5 %grad_kv.1 = (bf16[512,1024]{1,0:T(8,128)(2,1)S(1)}, bf16[512,1024]{1,0:T(8,128)(2,1)S(1)}, bf16[2,128,1024]{2,1,0:T(8,128)(2,1)S(1)}, bf16[2,128,1024]{2,1,0:T(8,128)(2,1)S(1)}) custom-call(s32[1,512]{1,0:T(1,128)S(1)} %bitcast.5, bf16[8,144,128]{2,1,0:T(8,128)(2,1)S(1)} %collective-permute-done.8.near_ref, ...), custom_call_target="tpu_custom_call" | custom-call | flops 32999999488 | bytes 1000000 | tf_op jit(solution)/shard_map/grad_kv/pallas_call | solution.py:541
  100.9 1.9 %collective-permute-start.10 = (bf16[2,128,1024]{2,1,0:T(8,128)(2,1)S(1)}, bf16[2,128,1024]{2,1,0:T(8,128)(2,1)S(1)}, u32[]{:S(2)}, u32[]{:S(2)}) collective-permute-start(bf16[2,128,1024]{2,1,0:T(8,128)(2,1)S(1)} %get-tuple-element.71), channel_id=1, source_target_pairs={{0,4},{4,8},{8,12},{12,16},{16,20},{20,24},{24,28},{1,5},{5,9},{9,... | collective-permute-start | bytes 1572872 | tf_op jit(solution)/shard_map/ppermute | solution.py:637
  102.8 4.3 %collective-permute-start.11 = (bf16[2,128,1024]{2,1,0:T(8,128)(2,1)S(1)}, bf16[2,128,1024]{2,1,0:T(8,128)(2,1)S(1)}, u32[]{:S(2)}, u32[]{:S(2)}) collective-permute-start(bf16[2,128,1024]{2,1,0:T(8,128)(2,1)S(1)} %get-tuple-element.72), channel_id=1, source_target_pairs={{4,0},{8,4},{12,8},{16,12},{20,16},{24,20},{28,24},{5,1},{9,5},{13... | collective-permute-start | bytes 1572872 | tf_op jit(solution)/shard_map/ppermute | solution.py:637
  107.1 1.6 %own.2.refs_0_ = bf16[512,1024]{1,0:T(8,128)(2,1)S(1)} custom-call(s32[1,512]{1,0:T(1,128)S(1)} %bitcast.6, bf16[512,1024]{1,0:T(8,128)(2,1)S(1)} %get-tuple-element.66.refs_0_, bf16[512,1024]{1,0:T(8,128)(2,1)S(1)} %get-tuple-element.70.refs_1_.refs_0_), custom_call_target="tpu_custom_call" | custom-call | flops 2200000000 | bytes 1000000 | tf_op jit(solution)/shard_map/own/pallas_call | solution.py:582
  108.7 9.4 %collective-permute-done.7.right_ref = bf16[1,128,1024]{2,1,0:T(8,128)(2,1)S(1)} collective-permute-done((bf16[1,128,1024]{2,1,0:T(8,128)(2,1)S(1)}, bf16[1,128,1024]{2,1,0:T(8,128)(2,1)S(1)}, u32[]{:S(2)}, u32[]{:S(2)}) %collective-permute-start.7) | collective-permute-done | bytes 262176 | tf_op jit(solution)/shard_map/ppermute | solution.py:637
  118.1 2.4 %finish.2.refs_2_ = bf16[512,1024]{1,0:T(8,128)(2,1)} custom-call(s32[2,128]{1,0:T(2,128)S(1)} %bitcast.9, bf16[1,128,1024]{2,1,0:T(8,128)(2,1)S(1)} %collective-permute-done.6.left_ref, bf16[1,128,1024]{2,1,0:T(8,128)(2,1)S(1)} %collective-permute-done.7.right_ref, bf16[512,1024]{1,0:T(8,128)(2,1)S(1)} %own.2.refs_0_), custom_call_target="tpu_custom_call" | custom-call | flops 2200000000 | bytes 1000000 | tf_op jit(solution)/shard_map/finish/pallas_call | solution.py:622
  120.4 3.0 %own.3 = (bf16[512,1024]{1,0:T(8,128)(2,1)S(1)}, bf16[512,1024]{1,0:T(8,128)(2,1)S(1)}) custom-call(s32[1,512]{1,0:T(1,128)S(1)} %bitcast.7, bf16[512,1024]{1,0:T(8,128)(2,1)S(1)} %get-tuple-element.70.refs_1_.refs_0_, bf16[512,1024]{1,0:T(8,128)(2,1)S(1)} %get-tuple-element.73.refs_1_, bf16[512,1024]{1,0:T(8,128)(2,1)} %finish.2.refs_2_), custom_call_target="tpu_custom_call" | custom-call | flops 2200000000 | bytes 1000000 | tf_op jit(solution)/shard_map/own/pallas_call | solution.py:582
  123.5 5.8 %collective-permute-done.11.right_ref = bf16[2,128,1024]{2,1,0:T(8,128)(2,1)S(1)} collective-permute-done((bf16[2,128,1024]{2,1,0:T(8,128)(2,1)S(1)}, bf16[2,128,1024]{2,1,0:T(8,128)(2,1)S(1)}, u32[]{:S(2)}, u32[]{:S(2)}) %collective-permute-start.11) | collective-permute-done | bytes 524320 | tf_op jit(solution)/shard_map/ppermute | solution.py:637
  129.3 2.9 %finish.3 = (bf16[512,1024]{1,0:T(8,128)(2,1)}, bf16[512,1024]{1,0:T(8,128)(2,1)}) custom-call(s32[2,128]{1,0:T(2,128)S(1)} %bitcast.10, bf16[2,128,1024]{2,1,0:T(8,128)(2,1)S(1)} %collective-permute-done.10.left_ref, bf16[2,128,1024]{2,1,0:T(8,128)(2,1)S(1)} %collective-permute-done.11.right_ref, bf16[512,1024]{1,0:T(8,128)(2,1)S(1)} %get-tuple-element.74.refs_0_, ...), custom_call_target="tpu_custom_call" | custom-call | flops 2200000000 | bytes 1000000 | tf_op jit(solution)/shard_map/finish/pallas_call | solution.py:622
  (16 shorter events, 0.0 us)
Async XLA Ops:
  0.6 10.4 %copy-start.4 = (f32[512,8]{0,1:T(8,128)S(1)}, f32[512,8]{0,1:T(8,128)}, u32[]{:S(2)}) copy-start(f32[512,8]{0,1:T(8,128)} %param.12) | copy-start | bytes 49156
  0.6 10.5 %copy-start = (s32[512]{0:T(512)S(1)}, s32[512]{0:T(512)}, u32[]{:S(2)}) copy-start(s32[512]{0:T(512)} %param.15) | copy-start | bytes 6148
  0.7 10.5 %copy-start.2 = (s32[8]{0:T(128)S(1)}, s32[8]{0:T(128)}, u32[]{:S(2)}) copy-start(s32[8]{0:T(128)} %docs_ref.1) | copy-start | bytes 100
  4.8 20.7 %collective-permute-start.2 = (bf16[2,128,1024]{2,1,0:T(8,128)(2,1)}, bf16[2,128,1024]{2,1,0:T(8,128)(2,1)S(1)}, u32[]{:S(2)}, u32[]{:S(2)}) collective-permute-start(bf16[2,128,1024]{2,1,0:T(8,128)(2,1)} %get-tuple-element.48), channel_id=1, source_target_pairs={{0,4},{4,8},{8,12},{12,16},{16,20},{20,24},{24,28},{1,5},{5,9},{9,... | collective-permute-start | bytes 1572872 | tf_op jit(solution)/shard_map/ppermute | solution.py:637
  8.0 30.5 %collective-permute-start.3 = (bf16[2,128,1024]{2,1,0:T(8,128)(2,1)}, bf16[2,128,1024]{2,1,0:T(8,128)(2,1)S(1)}, u32[]{:S(2)}, u32[]{:S(2)}) collective-permute-start(bf16[2,128,1024]{2,1,0:T(8,128)(2,1)} %get-tuple-element.49), channel_id=1, source_target_pairs={{4,0},{8,4},{12,8},{16,12},{20,16},{24,20},{28,24},{5,1},{9,5},{13... | collective-permute-start | bytes 1572872 | tf_op jit(solution)/shard_map/ppermute | solution.py:637
  19.4 26.9 %collective-permute-start = (bf16[1,128,1024]{2,1,0:T(8,128)(2,1)S(1)}, bf16[1,128,1024]{2,1,0:T(8,128)(2,1)S(1)}, u32[]{:S(2)}, u32[]{:S(2)}) collective-permute-start(bf16[1,128,1024]{2,1,0:T(8,128)(2,1)S(1)} %get-tuple-element.44), channel_id=1, source_target_pairs={{0,4},{4,8},{8,12},{12,16},{16,20},{20,24},{24,28},{1,5},{5,9},{9,... | collective-permute-start | bytes 786440 | tf_op jit(solution)/shard_map/ppermute | solution.py:637
  21.7 24.7 %collective-permute-start.1 = (bf16[1,128,1024]{2,1,0:T(8,128)(2,1)S(1)}, bf16[1,128,1024]{2,1,0:T(8,128)(2,1)S(1)}, u32[]{:S(2)}, u32[]{:S(2)}) collective-permute-start(bf16[1,128,1024]{2,1,0:T(8,128)(2,1)S(1)} %get-tuple-element.45), channel_id=1, source_target_pairs={{4,0},{8,4},{12,8},{16,12},{20,16},{24,20},{28,24},{5,1},{9,5},{13... | collective-permute-start | bytes 786440 | tf_op jit(solution)/shard_map/ppermute | solution.py:637
  43.1 10.7 %collective-permute-start.4 = (bf16[8,144,128]{2,1,0:T(8,128)(2,1)S(1)}, bf16[8,144,128]{2,1,0:T(8,128)(2,1)S(1)}, u32[]{:S(2)}, u32[]{:S(2)}) collective-permute-start(bf16[8,144,128]{2,1,0:T(8,128)(2,1)S(1)} %get-tuple-element.58), channel_id=1, source_target_pairs={{0,4},{4,8},{8,12},{12,16},{16,20},{20,24},{24,28},{1,5},{5,9},{9,... | collective-permute-start | bytes 884744 | tf_op jit(solution)/shard_map/ppermute | solution.py:637
  45.0 9.7 %collective-permute-start.5 = (bf16[8,144,128]{2,1,0:T(8,128)(2,1)S(1)}, bf16[8,144,128]{2,1,0:T(8,128)(2,1)S(1)}, u32[]{:S(2)}, u32[]{:S(2)}) collective-permute-start(bf16[8,144,128]{2,1,0:T(8,128)(2,1)S(1)} %get-tuple-element.58), channel_id=1, source_target_pairs={{0,8},{4,12},{8,16},{12,20},{16,24},{20,28},{1,9},{5,13},{9,17},{1... | collective-permute-start | bytes 884744 | tf_op jit(solution)/shard_map/ppermute | solution.py:637
  46.3 8.4 %copy-start.3 = (f32[8]{0:T(128)S(1)}, f32[8]{0:T(128)}, u32[]{:S(2)}) copy-start(f32[8]{0:T(128)} %scale_ref.3) | copy-start | bytes 100
  71.4 25.0 %collective-permute-start.8 = (bf16[8,144,128]{2,1,0:T(8,128)(2,1)S(1)}, bf16[8,144,128]{2,1,0:T(8,128)(2,1)S(1)}, u32[]{:S(2)}, u32[]{:S(2)}) collective-permute-start(bf16[8,144,128]{2,1,0:T(8,128)(2,1)S(1)} %get-tuple-element.67), channel_id=1, source_target_pairs={{4,0},{8,4},{12,8},{16,12},{20,16},{24,20},{28,24},{5,1},{9,5},{13... | collective-permute-start | bytes 884744 | tf_op jit(solution)/shard_map/ppermute | solution.py:637
  78.7 17.7 %collective-permute-start.9 = (bf16[8,144,128]{2,1,0:T(8,128)(2,1)S(1)}, bf16[8,144,128]{2,1,0:T(8,128)(2,1)S(1)}, u32[]{:S(2)}, u32[]{:S(2)}) collective-permute-start(bf16[8,144,128]{2,1,0:T(8,128)(2,1)S(1)} %get-tuple-element.67), channel_id=1, source_target_pairs={{8,0},{12,4},{16,8},{20,12},{24,16},{28,20},{9,1},{13,5},{17,9},{2... | collective-permute-start | bytes 884744 | tf_op jit(solution)/shard_map/ppermute | solution.py:637
  90.2 18.5 %collective-permute-start.6 = (bf16[1,128,1024]{2,1,0:T(8,128)(2,1)S(1)}, bf16[1,128,1024]{2,1,0:T(8,128)(2,1)S(1)}, u32[]{:S(2)}, u32[]{:S(2)}) collective-permute-start(bf16[1,128,1024]{2,1,0:T(8,128)(2,1)S(1)} %get-tuple-element.64), channel_id=1, source_target_pairs={{0,4},{4,8},{8,12},{12,16},{16,20},{20,24},{24,28},{1,5},{5,9},{9,... | collective-permute-start | bytes 786440 | tf_op jit(solution)/shard_map/ppermute | solution.py:637
  92.2 25.8 %collective-permute-start.7 = (bf16[1,128,1024]{2,1,0:T(8,128)(2,1)S(1)}, bf16[1,128,1024]{2,1,0:T(8,128)(2,1)S(1)}, u32[]{:S(2)}, u32[]{:S(2)}) collective-permute-start(bf16[1,128,1024]{2,1,0:T(8,128)(2,1)S(1)} %get-tuple-element.65), channel_id=1, source_target_pairs={{4,0},{8,4},{12,8},{16,12},{20,16},{24,20},{28,24},{5,1},{9,5},{13... | collective-permute-start | bytes 786440 | tf_op jit(solution)/shard_map/ppermute | solution.py:637
  100.9 22.6 %collective-permute-start.10 = (bf16[2,128,1024]{2,1,0:T(8,128)(2,1)S(1)}, bf16[2,128,1024]{2,1,0:T(8,128)(2,1)S(1)}, u32[]{:S(2)}, u32[]{:S(2)}) collective-permute-start(bf16[2,128,1024]{2,1,0:T(8,128)(2,1)S(1)} %get-tuple-element.71), channel_id=1, source_target_pairs={{0,4},{4,8},{8,12},{12,16},{16,20},{20,24},{24,28},{1,5},{5,9},{9,... | collective-permute-start | bytes 1572872 | tf_op jit(solution)/shard_map/ppermute | solution.py:637
  102.8 26.5 %collective-permute-start.11 = (bf16[2,128,1024]{2,1,0:T(8,128)(2,1)S(1)}, bf16[2,128,1024]{2,1,0:T(8,128)(2,1)S(1)}, u32[]{:S(2)}, u32[]{:S(2)}) collective-permute-start(bf16[2,128,1024]{2,1,0:T(8,128)(2,1)S(1)} %get-tuple-element.72), channel_id=1, source_target_pairs={{4,0},{8,4},{12,8},{16,12},{20,16},{24,20},{28,24},{5,1},{9,5},{13... | collective-permute-start | bytes 1572872 | tf_op jit(solution)/shard_map/ppermute | solution.py:637
  107.1 11.0 %copy-start.1 = (s32[1,2,128]{2,1,0:T(2,128)S(1)}, s32[1,2,128]{2,1,0:T(2,128)}, u32[]{:S(2)}) copy-start(s32[1,2,128]{2,1,0:T(2,128)} %param.14) | copy-start | bytes 3076
